TPU v7x, 32 devices: a whole 2x2x4 slice. The times are simulated.
32 devices in a mesh: seq: 4 (over z), chan: 4 (over y, x), dp: 2 (over core).
Axes of the slice: x: 2, y: 2, z: 4, core: 2. Of those that a mesh axis runs over, the one named last changes fastest.
Arguments:
- mr_query: bfloat16 [2, 8192, 512], P('dp', 'chan', 'seq'), may hold values from -6 to 6
- mr_key: bfloat16 [2, 8192, 512], P('dp', 'chan', 'seq'), may hold values from -6 to 6
- mr_value: bfloat16 [2, 8192, 512], P('dp', 'chan', 'seq'), may hold values from -6 to 6
- li_key: bfloat16 [2, 8192, 512], P('dp', 'chan', 'seq'), may hold values from -6 to 6
- li_value: bfloat16 [2, 8192, 512], P('dp', 'chan', 'seq'), may hold values from -6 to 6
- grad_out: bfloat16 [2, 8192, 512], P('dp', 'chan', 'seq'), may hold values from -6 to 6
- mr_filter: bfloat16 [512, 128], P('chan'), may hold values from -0.5 to 0.5
- li_residue: float32 [512, 16], P('chan'), may hold values from -1.5 to 1.5
- li_rate: float32 [512, 16], P('chan'), may hold values from 1.953125e-05 to 0.05
Outputs:
- grad_mr_query: bfloat16 [2, 8192, 512], P('dp', 'chan', 'seq')
- grad_mr_key: bfloat16 [2, 8192, 512], P('dp', 'chan', 'seq')
- grad_mr_value: bfloat16 [2, 8192, 512], P('dp', 'chan', 'seq')
- grad_li_key: bfloat16 [2, 8192, 512], P('dp', 'chan', 'seq')
- grad_li_value: bfloat16 [2, 8192, 512], P('dp', 'chan', 'seq')
- grad_filter: float32 [512, 128], P('chan')
- grad_residue: float32 [512, 16], P('chan')
All inputs are finite; a program needn't handle non-finite values.
Results may differ from a plain program's by a relative error of at most 0.012.
Values may be sent and summed in bfloat16 or wider, within the bound.
No kernel may reach another device: no remote copies, remote signals or barrier semaphores. Data moves between devices by JAX's collectives and lax.ppermute only.
A program may use at most 128 MiB of HBM per device.

v0:
```python
import functools

import jax
import jax.numpy as jnp
from jax import lax
from jax.experimental import pallas as pl
from jax.experimental.pallas import tpu as pltpu
from jax.sharding import PartitionSpec as P

F32 = jnp.float32
BF16 = jnp.bfloat16
TILE = 128
LANES = 16
PACK = TILE // LANES
CHUNK = 32
STEPS = 4
VMEM_LIMIT = 24 * 1024 * 1024


def nn(lhs, rhs):
    return lax.dot_general(lhs, rhs, (((1,), (0,)), ((), ())), preferred_element_type=F32)


def nt(lhs, rhs):
    return lax.dot_general(lhs, rhs, (((1,), (1,)), ((), ())), preferred_element_type=F32)


def iotas():
    rows = lax.broadcasted_iota(jnp.int32, (TILE, TILE), 0)
    cols = lax.broadcasted_iota(jnp.int32, (TILE, TILE), 1)
    return rows, cols


def ones_where(mask):
    return jnp.where(mask, 1.0, 0.0).astype(BF16)


def column(turned, mask):
    wide = jnp.concatenate([turned] * PACK, axis=0)
    return jnp.sum(jnp.where(mask, wide, 0.0), axis=1, keepdims=True)


def squeeze_groups(wide, mask):
    kept = jnp.where(mask, wide, 0.0)
    total = kept[:LANES]
    for g in range(1, PACK):
        total = total + kept[g * LANES : (g + 1) * LANES]
    return total


def spread_groups(narrow, mask):
    return jnp.where(mask, jnp.concatenate([narrow] * PACK, axis=0), 0.0)


def circulant(row):
    base = jnp.broadcast_to(row, (LANES, TILE))
    base = pltpu.roll(base, 0, 1, stride=1, stride_axis=0).astype(BF16)
    return jnp.concatenate(
        [base] + [pltpu.roll(base, LANES * j, 1) for j in range(1, PACK)], axis=0
    )


def reversal():
    rows, cols = iotas()
    return ones_where((rows + cols) % TILE == 0)


def one_minus_exp(value):
    series = jnp.full_like(value, 1.0)
    for order in (7, 6, 5, 4, 3, 2):
        series = 1.0 - value * series / order
    return jnp.where(value < 0.125, value * series, 1.0 - jnp.exp(-value))


def chunk_mask(shape, bit):
    return (lax.broadcasted_iota(jnp.int32, shape, 1) // CHUNK) & bit == 0


def pair_chunks(turned):
    parts = [turned[CHUNK * j : CHUNK * (j + 1), :] for j in range(TILE // CHUNK)]
    for bit in (1, 2):
        keep = chunk_mask((CHUNK, TILE), bit)
        for j in range(len(parts)):
            if j & bit == 0:
                low, high = parts[j], parts[j + bit]
                parts[j] = jnp.where(keep, low, pltpu.roll(high, CHUNK * bit, 1))
                parts[j + bit] = jnp.where(keep, pltpu.roll(low, TILE - CHUNK * bit, 1), high)
    return parts


def windows(before, now):
    lanes = lax.broadcasted_iota(jnp.int32, now.shape, 1)
    none = jnp.zeros_like(now)
    first, second = [none if before is None else before], [now]
    for j in range(1, TILE // CHUNK):
        left = TILE - CHUNK * j
        moved = pltpu.roll(now, left, 1)
        older = none if before is None else pltpu.roll(before, left, 1)
        first.append(jnp.where(lanes < left, older, moved))
        second.append(moved)
    return jnp.concatenate(
        [jnp.concatenate(first, axis=0), jnp.concatenate(second, axis=0)], axis=1
    )


def lag_rows(chunks, shifted_rows, own_rows):
    left = jnp.concatenate([chunks * own for own in own_rows], axis=0)
    wide = nn(left, shifted_rows)
    rows = lax.broadcasted_iota(jnp.int32, (2 * CHUNK, TILE), 0) % CHUNK
    lanes = lax.broadcasted_iota(jnp.int32, (2 * CHUNK, TILE), 1)
    sums = jnp.where(lanes + rows < CHUNK, wide[:, TILE:], wide[:, :TILE])
    sums = [
        pltpu.roll(sums[CHUNK * i : CHUNK * (i + 1)], 0, 1, stride=1, stride_axis=0)
        for i in range(2)
    ]
    return jnp.concatenate([jnp.sum(part, axis=0, keepdims=True) for part in sums], axis=0)


def crossed(left, weights):
    wide = nn(left, weights)
    return wide[:LANES, :TILE], wide[LANES:, TILE:]


def now_and_before(now, before, rows, half):
    pieces = []
    for g in range(PACK):
        part = slice(g * LANES, (g + 1) * LANES)
        circ = circulant(rows[g : g + 1, :])
        w_now = circ * half
        weights = jnp.concatenate([w_now, circ - w_now], axis=1)
        pair = crossed(jnp.concatenate([now[part, :], before[part, :]], axis=0), weights)
        pieces.append(pair[0] + pair[1])
    return jnp.concatenate(pieces, axis=0)


def within_shard(array, rows, half):
    pieces = []
    for g in range(0, PACK, 2):
        weights = [circulant(rows[h : h + 1, :]) * half for h in (g, g + 1)]
        part = slice(g * LANES, (g + 2) * LANES)
        pieces += crossed(array[part, :], jnp.concatenate(weights, axis=1))
    return jnp.concatenate(pieces, axis=0)


def block_groups(at, blocks, block):
    rows, cols = iotas()
    return cols == rows // LANES + (at * blocks + block) * PACK


def first_kernel(query, key, grad, value, rate, product, state):
    rows, cols = iotas()
    offsets = cols.astype(F32)
    mask = rows // LANES == cols // LANES
    at = pl.program_id(0)
    blocks = product.shape[0] // TILE
    for block in range(blocks):
        span = pl.ds(block * TILE, TILE)
        rates = column(rate[...], block_groups(at, blocks, block))
        powers = jnp.exp(-rates * offsets).astype(BF16)
        dz2 = grad[span, :] * value[span, :]
        state[:, span] = squeeze_groups(nt(powers, dz2), mask).astype(BF16)
        product[span, :] = query[span, :] * key[span, :]


def local_kernel(grad, value, rate, residue, du2, to_next, after, to_end, power, taps, decay):
    rows, cols = iotas()
    offsets = cols.astype(F32)
    mask = rows // LANES == cols // LANES
    lower_half = ones_where(rows >= cols)
    lags = ((CHUNK - 1 - cols) % TILE).astype(F32)
    at = pl.program_id(0)
    blocks = grad.shape[0] // TILE
    filters = []
    for block in range(blocks):
        span = pl.ds(block * TILE, TILE)
        own = block_groups(at, blocks, block)
        rates = column(rate[...], own)
        gains = jnp.sqrt(one_minus_exp(2.0 * rates))
        coeffs = column(residue[...], own) * gains
        powers = jnp.exp(-rates * offsets)
        ends = jnp.exp(-rates * (TILE - 1 - offsets))
        stepped = coeffs * jnp.exp(-rates)
        power[span, :] = jnp.exp(-rates * lags).astype(BF16)
        to_end[span, :] = ends.astype(BF16)
        after[span, :] = (powers * stepped).astype(BF16)
        to_next[span, :] = (ends * stepped).astype(BF16)
        fades = jnp.broadcast_to(jnp.exp(-rates * TILE), (TILE, TILE))
        decay[:, span] = squeeze_groups(fades, mask)
        filters.append(jnp.sum((powers * coeffs).reshape(PACK, LANES, TILE), axis=1))
    filters = jnp.concatenate(filters, axis=0)
    taps[...] = filters
    turned = nn(filters.astype(BF16), reversal())
    for block in range(blocks):
        span = pl.ds(block * TILE, TILE)
        dz2 = grad[span, :] * value[span, :]
        du2[span, :] = within_shard(dz2, turned[block * PACK : (block + 1) * PACK], lower_half)


def middle_kernel(count, *refs):
    states = refs[: count - 1]
    local, to_next, decay, li_key, value, dz1, du2, after_shard = refs[count - 1 :]
    rows, cols = iotas()
    mask = rows // LANES == cols // LANES
    for block in range(local.shape[0] // TILE):
        span = pl.ds(block * TILE, TILE)
        fade = decay[:, span]
        carried = states[-1][:, span].astype(F32)
        for state in states[-2::-1]:
            carried = state[:, span].astype(F32) + fade * carried
        after_shard[:, span] = carried
        wide = spread_groups(carried, mask).T.astype(BF16)
        total = local[span, :] + nn(wide, to_next[span, :])
        du2[span, :] = total
        dy1 = total * li_key[span, :].astype(F32)
        dz1[span, :] = (dy1 * value[span, :].astype(F32)).astype(BF16)


def forward_kernel(
    before, now, filters, value, li_key, to_end, du2, grad_value, grad_key, u2, state
):
    rows, cols = iotas()
    mask = rows // LANES == cols // LANES
    upper_half = ones_where(cols >= rows)
    for block in range(now.shape[0] // TILE):
        span = pl.ds(block * TILE, TILE)
        filt = filters[pl.ds(block * PACK, PACK), :].astype(F32)
        z1 = now_and_before(now[span, :], before[span, :], filt, upper_half)
        y1 = (value[span, :].astype(F32) * z1).astype(BF16).astype(F32)
        key_two = li_key[span, :].astype(F32)
        u2_half = (y1 * key_two).astype(BF16)
        u2[span, :] = u2_half
        state[:, span] = squeeze_groups(nt(to_end[span, :], u2_half), mask).astype(BF16)
        du2_here = du2[span, :]
        grad_key[span, :] = (du2_here * y1).astype(BF16)
        grad_value[span, :] = (du2_here * key_two * z1).astype(BF16)


def sums_kernel(
    before, now, u2, dz1, grad, li_value, power, state, after_shard, rate,
    packed, filter_sums, within_sums, across_sums,
):
    rows, cols = iotas()
    turn = ones_where(cols == rows - rows % CHUNK + (CHUNK - 1 - rows % CHUNK))
    lanes = lax.broadcasted_iota(jnp.int32, (CHUNK, TILE), 1)
    own_rows = [ones_where((lanes // LANES) % 2 == i) for i in range(2)]
    at = pl.program_id(0)
    blocks = now.shape[0] // TILE

    @pl.when(at == 0)
    def _():
        within_sums[...] = jnp.zeros_like(within_sums)
        across_sums[...] = jnp.zeros_like(across_sums)

    for block in range(blocks):
        span = pl.ds(block * TILE, TILE)
        dz2 = grad[span, :] * li_value[span, :]
        turned = nt(turn, jnp.concatenate([dz1[span, :], dz2], axis=0)).astype(BF16)
        lag_chunks = pair_chunks(turned[:, :TILE])
        energy_chunks = pair_chunks(turned[:, TILE:])
        lags, energies = [], []
        for p in range(TILE // CHUNK):
            pair = pl.ds(block * TILE + p * CHUNK, CHUNK)
            lags.append(lag_rows(lag_chunks[p], windows(before[pair, :], now[pair, :]), own_rows))
            energies.append(lag_rows(energy_chunks[p], windows(None, u2[pair, :]), own_rows))
        few = pl.ds(pl.multiple_of((at * blocks + block) * PACK, PACK), PACK)
        filter_sums[few, :] = jnp.concatenate(lags, axis=0)
        energies = jnp.concatenate(energies, axis=0).astype(BF16)
        energies = jnp.concatenate([energies] * LANES, axis=0)
        own = block_groups(at, blocks, block)
        within_sums[...] += squeeze_groups(nt(power[span, :], energies), own)
        across = state[:, span].astype(F32) * after_shard[:, span]
        across_sums[...] += nn(across.astype(BF16), ones_where(own))

    @pl.when(at == STEPS - 1)
    def _():
        place = ones_where((rows + cols) % TILE == CHUNK - 1)
        sums = nn(filter_sums[...].astype(BF16), place).astype(BF16)
        for chunk in range(filter_sums.shape[0] // LANES):
            packed[chunk] = sums[chunk * LANES : (chunk + 1) * LANES]
        rates = rate[...]
        gains = jnp.sqrt(one_minus_exp(2.0 * rates))
        total = gains * (within_sums[...] + jnp.exp(-rates) * across_sums[...])
        packed[filter_sums.shape[0] // LANES] = total.astype(BF16)


def within_kernel(u2, taps, z2):
    rows, cols = iotas()
    upper_half = ones_where(cols >= rows)
    for block in range(u2.shape[0] // TILE):
        span = pl.ds(block * TILE, TILE)
        z2[span, :] = within_shard(u2[span, :], taps[pl.ds(block * PACK, PACK), :], upper_half)


def last_kernel(half, other, grad_filter, grad_residue):
    chunks = half.shape[0] - 1
    for chunk in range(chunks):
        grad_filter[pl.ds(chunk * LANES, LANES), :] = half[chunk].astype(F32) + other[chunk].astype(F32)
    grad_residue[...] = half[chunks].astype(F32) + other[chunks].astype(F32)


def product_kernel(dz1, later, filters, query, key, grad_query, grad_key):
    rows, cols = iotas()
    lower_half = ones_where(rows >= cols)
    turned = nn(filters[...], reversal())
    for block in range(dz1.shape[0] // TILE):
        span = pl.ds(block * TILE, TILE)
        filt = turned[block * PACK : (block + 1) * PACK]
        du1 = now_and_before(dz1[span, :], later[span, :], filt, lower_half)
        grad_query[span, :] = (du1 * key[span, :].astype(F32)).astype(BF16)
        grad_key[span, :] = (du1 * query[span, :].astype(F32)).astype(BF16)


def value_kernel(count, *refs):
    states = refs[: count - 1]
    after, decay, z2, grad, grad_value = refs[count - 1 :]
    rows, cols = iotas()
    mask = rows // LANES == cols // LANES
    for block in range(z2.shape[0] // TILE):
        span = pl.ds(block * TILE, TILE)
        fade = decay[:, span]
        carried = states[-1][:, span].astype(F32)
        for state in states[-2::-1]:
            carried = state[:, span].astype(F32) + fade * carried
        wide = spread_groups(carried, mask).T.astype(BF16)
        total = z2[span, :] + nn(wide, after[span, :])
        grad_value[span, :] = (grad[span, :].astype(F32) * total).astype(BF16)


def shifted(value, axis, steps):
    count = lax.axis_size(axis)
    first, last = max(0, -steps), min(count, count - steps)
    return lax.ppermute(value, axis, [(source, source + steps) for source in range(first, last)])


def exchanged(half, axes, beside):
    partners = []
    for axis in axes:
        count, bit = lax.axis_size(axis), 1
        assert count & (count - 1) == 0
        while bit < count:
            partners.append((axis, [(source, source ^ bit) for source in range(count)]))
            bit *= 2
    made = []
    for at, (axis, pairs) in enumerate(partners):
        other = lax.ppermute(half, axis, pairs)
        if at < len(partners) - 1:
            half = (half.astype(F32) + other.astype(F32)).astype(BF16)
            if at < len(beside):
                half, arrays = lax.optimization_barrier((half, beside[at]))
                made.append(arrays)
    return half, other, made


def per_device(
    mr_query, mr_key, mr_value, li_key, li_value, grad_out, mr_filter, li_residue, li_rate
):
    query, key, value, key_two, value_two, grad = (
        array[0] for array in (mr_query, mr_key, mr_value, li_key, li_value, grad_out)
    )
    groups, filt_len = mr_filter.shape
    channels, seq_local = query.shape
    assert filt_len == TILE and seq_local == TILE and groups <= TILE
    assert channels == groups * LANES and li_rate.shape[1] == LANES
    count = lax.axis_size("seq")
    rows = channels // STEPS
    few = groups // STEPS
    spare = ((0, 0), (0, TILE - groups))
    rate = jnp.pad(li_rate.T, spare)
    residue = jnp.pad(li_residue.T, spare)

    wide = pl.BlockSpec((rows, TILE), lambda i: (i, 0))
    table = pl.BlockSpec((few, TILE), lambda i: (i, 0))
    narrow = pl.BlockSpec((LANES, rows), lambda i: (0, i))
    modes = pl.BlockSpec((LANES, TILE), lambda i: (0, 0))
    wide_half = jax.ShapeDtypeStruct((channels, TILE), BF16)
    wide_full = jax.ShapeDtypeStruct((channels, TILE), F32)
    narrow_half = jax.ShapeDtypeStruct((LANES, channels), BF16)
    narrow_full = jax.ShapeDtypeStruct((LANES, channels), F32)

    def call(kernel, name, in_specs, out_specs, out_shape, scratch=(), limit=VMEM_LIMIT, grid=STEPS):
        return pl.pallas_call(
            kernel,
            grid=(grid,),
            in_specs=in_specs,
            out_specs=out_specs,
            out_shape=out_shape,
            scratch_shapes=scratch,
            name=name,
            cost_estimate=pl.CostEstimate(flops=1, bytes_accessed=1, transcendentals=0),
            compiler_params=pltpu.CompilerParams(vmem_limit_bytes=limit),
        )

    product, back = call(
        first_kernel, "first",
        [wide] * 4 + [modes], [wide, narrow], [wide_half, narrow_half], limit=60 * 1024 * 1024,
    )(query, key, grad, value_two, rate)
    product_before = shifted(product, "seq", 1)
    later_backs = [shifted(back, "seq", -gap) for gap in range(1, count)]

    du2_local, to_next, after, to_end, power, taps, decay = call(
        local_kernel, "local",
        [wide, wide, modes, modes],
        [wide] * 5 + [table, narrow],
        [wide_full] + [wide_half] * 4 + [jax.ShapeDtypeStruct((groups, TILE), F32), narrow_full],
    )(grad, value_two, rate, residue)

    dz1, du2, after_shard = call(
        functools.partial(middle_kernel, count), "middle",
        [narrow] * (count - 1) + [wide, wide, narrow, wide, wide],
        [wide, wide, narrow], [wide_half, wide_full, narrow_full],
    )(*later_backs, du2_local, to_next, decay, key_two, value)
    dz1_later = shifted(dz1, "seq", -1)

    grad_mr_value, grad_li_key, u2, state = call(
        forward_kernel, "forward",
        [wide, wide, table, wide, wide, wide, wide],
        [wide, wide, wide, narrow], [wide_half] * 3 + [narrow_half],
    )(product_before, product, mr_filter, value, key_two, to_end, du2)
    earlier_states = [shifted(state, "seq", gap) for gap in range(1, count)]

    chunks = groups // LANES + 1
    whole = pl.BlockSpec((chunks, LANES, TILE), lambda i: (0, 0, 0))
    (packed,) = call(
        sums_kernel, "sums",
        [wide] * 7 + [narrow, narrow, modes],
        [whole], [jax.ShapeDtypeStruct((chunks, LANES, TILE), BF16)],
        [pltpu.VMEM((groups, TILE), F32)] + [pltpu.VMEM((LANES, TILE), F32)] * 2,
    )(product_before, product, u2, dz1, grad, value_two, power, state, after_shard, rate)
    packed, dz1_later, *earlier_states = lax.optimization_barrier(
        (packed, dz1_later, *earlier_states)
    )

    (z2,) = call(within_kernel, "within", [wide, table], [wide], [wide_full])(u2, taps)

    products = call(
        product_kernel, "product",
        [wide, wide, table, wide, wide], [wide, wide], [wide_half, wide_half],
    )(dz1, dz1_later, mr_filter, query, key)

    half, other, ((z2,), (grad_query, grad_key)) = exchanged(
        packed, ("dp", "seq"), [[z2], products]
    )

    (grad_li_value,) = call(
        functools.partial(value_kernel, count), "value",
        [narrow] * (count - 1) + [wide, narrow, wide, wide], [wide], [wide_half],
    )(*earlier_states, after, decay, z2, grad)

    all_groups = pl.BlockSpec((groups, TILE), lambda i: (0, 0))
    grad_filter, grad_residue = call(
        last_kernel, "last", [whole, whole], [all_groups, modes],
        [jax.ShapeDtypeStruct((groups, TILE), F32), jax.ShapeDtypeStruct((LANES, TILE), F32)],
        grid=1,
    )(half, other)
    return (
        grad_query[None],
        grad_key[None],
        grad_mr_value[None],
        grad_li_key[None],
        grad_li_value[None],
        grad_filter,
        grad_residue[:, :groups].T,
    )


def solution(mesh):
    streams = (P("dp", "chan", "seq"),)
    tables = (P("chan", None),)
    return jax.shard_map(
        per_device,
        mesh=mesh,
        in_specs=streams * 6 + tables * 3,
        out_specs=streams * 5 + tables * 2,
        check_vma=False,
    )
```

profile of v0, /device:TPU:0, one launch (start us, length us, event | category | flops | bytes accessed | tf_op | source)
XLA Modules:
  0.0 62.4 jit_solution(14988781287685312857)
XLA Ops:
  0.6 0.0 copy-start
  0.6 0.0 copy-start.1
  0.7 0.0 copy-start.8
  0.7 0.0 copy-start.9
  0.7 4.1 %first.1 = (bf16[2048,128]{1,0:T(8,128)(2,1)}, bf16[16,2048]{1,0:T(8,128)(2,1)}) custom-call(bf16[2048,128]{1,0:T(8,128)(2,1)} %bitcast.25, bf16[2048,128]{1,0:T(8,128)(2,1)} %bitcast.27, bf16[2048,128]{1,0:T(8,128)(2,1)} %bitcast.14, bf16[2048,128]{1,0:T(8,128)(2,1)} %bitcast.18, f32[16,128]{1,0:T(8,128)} %bitcast.29), custom_call_target="tpu_custom_call" | custom-call | flops 1 | bytes 1 | tf_op jit(solution)/shard_map/first/pallas_call | solution.py:393
  4.7 1.3 %collective-permute-start.1 = (bf16[16,2048]{1,0:T(8,128)(2,1)}, bf16[16,2048]{1,0:T(8,128)(2,1)S(1)}, u32[]{:S(2)}, u32[]{:S(2)}) collective-permute-start(bf16[16,2048]{1,0:T(8,128)(2,1)} %get-tuple-element.39), channel_id=1, source_target_pairs={{8,0},{16,8},{24,16},{9,1},{17,9},{25,17},{10,2},{18,10},{26,18},{... | collective-permute-start | bytes 196616 | tf_op jit(solution)/shard_map/ppermute | solution.py:332
  6.0 1.3 %collective-permute-start.2 = (bf16[16,2048]{1,0:T(8,128)(2,1)}, bf16[16,2048]{1,0:T(8,128)(2,1)S(1)}, u32[]{:S(2)}, u32[]{:S(2)}) collective-permute-start(bf16[16,2048]{1,0:T(8,128)(2,1)} %get-tuple-element.39), channel_id=1, source_target_pairs={{16,0},{24,8},{17,1},{25,9},{18,2},{26,10},{19,3},{27,11},{20,4},{... | collective-permute-start | bytes 196616 | tf_op jit(solution)/shard_map/ppermute | solution.py:332
  7.3 1.3 %collective-permute-start.3 = (bf16[16,2048]{1,0:T(8,128)(2,1)}, bf16[16,2048]{1,0:T(8,128)(2,1)S(1)}, u32[]{:S(2)}, u32[]{:S(2)}) collective-permute-start(bf16[16,2048]{1,0:T(8,128)(2,1)} %get-tuple-element.39), channel_id=1, source_target_pairs={{24,0},{25,1},{26,2},{27,3},{28,4},{29,5},{30,6},{31,7}} | collective-permute-start | bytes 196616 | tf_op jit(solution)/shard_map/ppermute | solution.py:332
  8.6 5.0 %collective-permute-start = (bf16[2048,128]{1,0:T(8,128)(2,1)}, bf16[2048,128]{1,0:T(8,128)(2,1)S(1)}, u32[]{:S(2)}, u32[]{:S(2)}) collective-permute-start(bf16[2048,128]{1,0:T(8,128)(2,1)} %get-tuple-element.37.now), channel_id=1, source_target_pairs={{0,8},{8,16},{16,24},{1,9},{9,17},{17,25},{2,10},{10,18},{18,26},{... | collective-permute-start | bytes 1572872 | tf_op jit(solution)/shard_map/ppermute | solution.py:332
  13.6 0.0 copy-done
  13.6 0.0 copy-done.1
  13.6 0.0 copy-done.8
  13.6 0.0 copy-done.9
  13.6 0.0 copy-start.3
  13.7 0.0 copy-start.4
  13.7 5.5 %local.1 = (f32[2048,128]{1,0:T(8,128)S(1)}, bf16[2048,128]{1,0:T(8,128)(2,1)S(1)}, bf16[2048,128]{1,0:T(8,128)(2,1)S(1)}, bf16[2048,128]{1,0:T(8,128)(2,1)S(1)}...) custom-call(bf16[2048,128]{1,0:T(8,128)(2,1)S(1)} %bitcast.15, ...), custom_call_target="tpu_custom_call" | custom-call | flops 1 | bytes 1 | tf_op jit(solution)/shard_map/local/pallas_call | solution.py:400
  19.2 0.0 collective-permute-done.1.refs_0_
  19.2 0.0 collective-permute-done.2.refs_1_
  19.2 0.0 collective-permute-done.3.refs_2_
  19.2 0.0 copy-done.3
  19.2 0.0 copy-done.4
  19.2 0.0 copy-start.2
  19.2 0.0 copy-start.7
  19.2 1.2 %middle.1 = (bf16[2048,128]{1,0:T(8,128)(2,1)S(1)}, f32[2048,128]{1,0:T(8,128)S(1)}, f32[16,2048]{1,0:T(8,128)S(1)}) custom-call(bf16[16,2048]{1,0:T(8,128)(2,1)S(1)} %collective-permute-done.1.refs_0_, bf16[16,2048]{1,0:T(8,128)(2,1)S(1)} %collective-permute-done.2.refs_1_, bf16[16,2048]{1,0:T(8,128)(2,1)S(1)} %collective-permute-done.3.refs_2_, ...), custom_call_target="tpu_custom_call" | custom-call | flops 1 | bytes 1 | tf_op jit(solution)/shard_map/middle/pallas_call | solution.py:407
  20.4 1.3 %collective-permute-start.4 = (bf16[2048,128]{1,0:T(8,128)(2,1)S(1)}, bf16[2048,128]{1,0:T(8,128)(2,1)S(1)}, u32[]{:S(2)}, u32[]{:S(2)}) collective-permute-start(bf16[2048,128]{1,0:T(8,128)(2,1)S(1)} %get-tuple-element.45.dz1), channel_id=1, source_target_pairs={{8,0},{16,8},{24,16},{9,1},{17,9},{25,17},{10,2},{18,10},{26,18},{... | collective-permute-start | bytes 1572872 | tf_op jit(solution)/shard_map/ppermute | solution.py:332
  21.7 3.3 %collective-permute-done.before = bf16[2048,128]{1,0:T(8,128)(2,1)S(1)} collective-permute-done((bf16[2048,128]{1,0:T(8,128)(2,1)}, bf16[2048,128]{1,0:T(8,128)(2,1)S(1)}, u32[]{:S(2)}, u32[]{:S(2)}) %collective-permute-start) | collective-permute-done | bytes 524320 | tf_op jit(solution)/shard_map/ppermute | solution.py:332
  25.1 0.0 copy-done.2
  25.1 5.0 %forward.1 = (bf16[2048,128]{1,0:T(8,128)(2,1)}, bf16[2048,128]{1,0:T(8,128)(2,1)}, bf16[2048,128]{1,0:T(8,128)(2,1)S(1)}, bf16[16,2048]{1,0:T(8,128)(2,1)S(1)}) custom-call(bf16[2048,128]{1,0:T(8,128)(2,1)S(1)} %collective-permute-done.before, bf16[2048,128]{1,0:T(8,128)(2,1)S(1)} %copy-done.2, bf16[128,128]{1,0:T(8,128)(2,1)S(1)} %copy-done.7, ...), custom_call_target="tpu_custom_call" | custom-call | flops 1 | bytes 1 | tf_op jit(solution)/shard_map/forward/pallas_call | solution.py:414
  30.0 4.3 %collective-permute-start.5 = (bf16[16,2048]{1,0:T(8,128)(2,1)S(1)}, bf16[16,2048]{1,0:T(8,128)(2,1)S(1)}, u32[]{:S(2)}, u32[]{:S(2)}) collective-permute-start(bf16[16,2048]{1,0:T(8,128)(2,1)S(1)} %get-tuple-element.47.state), channel_id=1, source_target_pairs={{0,8},{8,16},{16,24},{1,9},{9,17},{17,25},{2,10},{10,18},{18,26},{... | collective-permute-start | bytes 196616 | tf_op jit(solution)/shard_map/ppermute | solution.py:332
  34.3 5.8 %collective-permute-start.6 = (bf16[16,2048]{1,0:T(8,128)(2,1)S(1)}, bf16[16,2048]{1,0:T(8,128)(2,1)S(1)}, u32[]{:S(2)}, u32[]{:S(2)}) collective-permute-start(bf16[16,2048]{1,0:T(8,128)(2,1)S(1)} %get-tuple-element.47.state), channel_id=1, source_target_pairs={{0,16},{8,24},{1,17},{9,25},{2,18},{10,26},{3,19},{11,27},{4,20},{... | collective-permute-start | bytes 196616 | tf_op jit(solution)/shard_map/ppermute | solution.py:332
  40.2 1.3 %collective-permute-start.7 = (bf16[16,2048]{1,0:T(8,128)(2,1)S(1)}, bf16[16,2048]{1,0:T(8,128)(2,1)S(1)}, u32[]{:S(2)}, u32[]{:S(2)}) collective-permute-start(bf16[16,2048]{1,0:T(8,128)(2,1)S(1)} %get-tuple-element.47.state), channel_id=1, source_target_pairs={{0,24},{1,25},{2,26},{3,27},{4,28},{5,29},{6,30},{7,31}} | collective-permute-start | bytes 196616 | tf_op jit(solution)/shard_map/ppermute | solution.py:332
  41.5 8.3 %sums.1 = bf16[9,16,128]{2,1,0:T(8,128)(2,1)S(1)} custom-call(bf16[2048,128]{1,0:T(8,128)(2,1)S(1)} %collective-permute-done.before, bf16[2048,128]{1,0:T(8,128)(2,1)S(1)} %copy-done.2, bf16[2048,128]{1,0:T(8,128)(2,1)S(1)} %get-tuple-element.44.u2, bf16[2048,128]{1,0:T(8,128)(2,1)S(1)} %get-tuple-element.45.dz1, bf16[2048,128]{1,0:T(8,128)(2,1)S(1)} %bitcast.16, ...), custom_call_target="tpu_custom_call" | custom-call | flops 1 | bytes 1 | tf_op jit(solution)/shard_map/sums/pallas_call | solution.py:423
  49.7 0.0 collective-permute-done.5.refs_0_
  49.8 0.0 collective-permute-done.6.refs_1_
  49.8 0.0 collective-permute-done.7.refs_2_
  49.8 0.0 collective-permute-done.4.later
  49.8 0.1 collective-permute-start.8
  49.9 0.0 copy-start.5
  49.9 0.0 copy-start.6
  49.9 2.4 %within.1.refs_5_ = f32[2048,128]{1,0:T(8,128)S(1)} custom-call(bf16[2048,128]{1,0:T(8,128)(2,1)S(1)} %get-tuple-element.44.u2, f32[128,128]{1,0:T(8,128)S(1)} %get-tuple-element.50.taps), custom_call_target="tpu_custom_call" | custom-call | flops 1 | bytes 1 | tf_op jit(solution)/shard_map/within/pallas_call | solution.py:433
  52.3 0.0 collective-permute-done.8
  52.4 0.1 collective-permute-start.9
  52.5 4.3 %product.1 = (bf16[2048,128]{1,0:T(8,128)(2,1)}, bf16[2048,128]{1,0:T(8,128)(2,1)}) custom-call(bf16[2048,128]{1,0:T(8,128)(2,1)S(1)} %get-tuple-element.45.dz1, bf16[2048,128]{1,0:T(8,128)(2,1)S(1)} %collective-permute-done.4.later, bf16[128,128]{1,0:T(8,128)(2,1)S(1)} %copy-done.7, bf16[2048,128]{1,0:T(8,128)(2,1)S(1)} %bitcast.26, ...), custom_call_target="tpu_custom_call" | custom-call | flops 1 | bytes 1 | tf_op jit(solution)/shard_map/product/pallas_call | solution.py:435
  56.8 0.0 collective-permute-done.9
  56.8 0.1 collective-permute-start.10
  56.9 2.2 %value.1 = bf16[2048,128]{1,0:T(8,128)(2,1)} custom-call(bf16[16,2048]{1,0:T(8,128)(2,1)S(1)} %collective-permute-done.5.refs_0_, bf16[16,2048]{1,0:T(8,128)(2,1)S(1)} %collective-permute-done.6.refs_1_, bf16[16,2048]{1,0:T(8,128)(2,1)S(1)} %collective-permute-done.7.refs_2_, bf16[2048,128]{1,0:T(8,128)(2,1)S(1)} %get-tuple-element.62.refs_3_, ...), custom_call_target="tpu_custom_call" | custom-call | flops 1 | bytes 1 | tf_op jit(solution)/shard_map/value/pallas_call | solution.py:444
  59.1 2.7 %collective-permute-done.10.other = bf16[9,16,128]{2,1,0:T(8,128)(2,1)S(1)} collective-permute-done((bf16[9,16,128]{2,1,0:T(8,128)(2,1)S(1)}, bf16[9,16,128]{2,1,0:T(8,128)(2,1)S(1)}, u32[]{:S(2)}, u32[]{:S(2)}) %collective-permute-start.10) | collective-permute-done | bytes 36896 | tf_op jit(solution)/shard_map/ppermute | solution.py:345
  61.7 0.6 %last.1 = (f32[128,128]{1,0:T(8,128)}, f32[16,128]{1,0:T(8,128)}) custom-call(bf16[9,16,128]{2,1,0:T(8,128)(2,1)S(1)} %add_convert_fusion.half, bf16[9,16,128]{2,1,0:T(8,128)(2,1)S(1)} %collective-permute-done.10.other), custom_call_target="tpu_custom_call" | custom-call | flops 1 | bytes 1 | tf_op jit(solution)/shard_map/last/pallas_call | solution.py:450
  (5 shorter events, 0.0 us)
Async XLA Ops:
  0.6 13.0 %copy-start = (bf16[1,2048,128]{2,1,0:T(8,128)(2,1)S(1)}, bf16[1,2048,128]{2,1,0:T(8,128)(2,1)}, u32[]{:S(2)}) copy-start(bf16[1,2048,128]{2,1,0:T(8,128)(2,1)} %param.14) | copy-start | bytes 1572868
  0.6 13.0 %copy-start.1 = (bf16[1,2048,128]{2,1,0:T(8,128)(2,1)S(1)}, bf16[1,2048,128]{2,1,0:T(8,128)(2,1)}, u32[]{:S(2)}) copy-start(bf16[1,2048,128]{2,1,0:T(8,128)(2,1)} %param.13) | copy-start | bytes 1572868
  0.7 13.0 %copy-start.8 = (f32[128,16]{0,1:T(8,128)S(1)}, f32[128,16]{0,1:T(8,128)}, u32[]{:S(2)}) copy-start(f32[128,16]{0,1:T(8,128)} %param.17) | copy-start | bytes 24580
  0.7 13.0 %copy-start.9 = (f32[128,16]{0,1:T(8,128)S(1)}, f32[128,16]{0,1:T(8,128)}, u32[]{:S(2)}) copy-start(f32[128,16]{0,1:T(8,128)} %param.16) | copy-start | bytes 24580
  4.7 14.4 %collective-permute-start.1 = (bf16[16,2048]{1,0:T(8,128)(2,1)}, bf16[16,2048]{1,0:T(8,128)(2,1)S(1)}, u32[]{:S(2)}, u32[]{:S(2)}) collective-permute-start(bf16[16,2048]{1,0:T(8,128)(2,1)} %get-tuple-element.39), channel_id=1, source_target_pairs={{8,0},{16,8},{24,16},{9,1},{17,9},{25,17},{10,2},{18,10},{26,18},{... | collective-permute-start | bytes 196616 | tf_op jit(solution)/shard_map/ppermute | solution.py:332
  6.0 13.1 %collective-permute-start.2 = (bf16[16,2048]{1,0:T(8,128)(2,1)}, bf16[16,2048]{1,0:T(8,128)(2,1)S(1)}, u32[]{:S(2)}, u32[]{:S(2)}) collective-permute-start(bf16[16,2048]{1,0:T(8,128)(2,1)} %get-tuple-element.39), channel_id=1, source_target_pairs={{16,0},{24,8},{17,1},{25,9},{18,2},{26,10},{19,3},{27,11},{20,4},{... | collective-permute-start | bytes 196616 | tf_op jit(solution)/shard_map/ppermute | solution.py:332
  7.3 11.9 %collective-permute-start.3 = (bf16[16,2048]{1,0:T(8,128)(2,1)}, bf16[16,2048]{1,0:T(8,128)(2,1)S(1)}, u32[]{:S(2)}, u32[]{:S(2)}) collective-permute-start(bf16[16,2048]{1,0:T(8,128)(2,1)} %get-tuple-element.39), channel_id=1, source_target_pairs={{24,0},{25,1},{26,2},{27,3},{28,4},{29,5},{30,6},{31,7}} | collective-permute-start | bytes 196616 | tf_op jit(solution)/shard_map/ppermute | solution.py:332
  8.6 16.4 %collective-permute-start = (bf16[2048,128]{1,0:T(8,128)(2,1)}, bf16[2048,128]{1,0:T(8,128)(2,1)S(1)}, u32[]{:S(2)}, u32[]{:S(2)}) collective-permute-start(bf16[2048,128]{1,0:T(8,128)(2,1)} %get-tuple-element.37.now), channel_id=1, source_target_pairs={{0,8},{8,16},{16,24},{1,9},{9,17},{17,25},{2,10},{10,18},{18,26},{... | collective-permute-start | bytes 1572872 | tf_op jit(solution)/shard_map/ppermute | solution.py:332
  13.6 5.6 %copy-start.3 = (bf16[1,2048,128]{2,1,0:T(8,128)(2,1)S(1)}, bf16[1,2048,128]{2,1,0:T(8,128)(2,1)}, u32[]{:S(2)}) copy-start(bf16[1,2048,128]{2,1,0:T(8,128)(2,1)} %param.12) | copy-start | bytes 1572868
  13.7 5.6 %copy-start.4 = (bf16[1,2048,128]{2,1,0:T(8,128)(2,1)S(1)}, bf16[1,2048,128]{2,1,0:T(8,128)(2,1)}, u32[]{:S(2)}) copy-start(bf16[1,2048,128]{2,1,0:T(8,128)(2,1)} %param.11) | copy-start | bytes 1572868
  19.2 5.8 %copy-start.2 = (bf16[2048,128]{1,0:T(8,128)(2,1)S(1)}, bf16[2048,128]{1,0:T(8,128)(2,1)}, u32[]{:S(2)}) copy-start(bf16[2048,128]{1,0:T(8,128)(2,1)} %get-tuple-element.37.now) | copy-start | bytes 1572868
  19.2 5.8 %copy-start.7 = (bf16[128,128]{1,0:T(8,128)(2,1)S(1)}, bf16[128,128]{1,0:T(8,128)(2,1)}, u32[]{:S(2)}) copy-start(bf16[128,128]{1,0:T(8,128)(2,1)} %filters.3) | copy-start | bytes 98308
  20.4 29.3 %collective-permute-start.4 = (bf16[2048,128]{1,0:T(8,128)(2,1)S(1)}, bf16[2048,128]{1,0:T(8,128)(2,1)S(1)}, u32[]{:S(2)}, u32[]{:S(2)}) collective-permute-start(bf16[2048,128]{1,0:T(8,128)(2,1)S(1)} %get-tuple-element.45.dz1), channel_id=1, source_target_pairs={{8,0},{16,8},{24,16},{9,1},{17,9},{25,17},{10,2},{18,10},{26,18},{... | collective-permute-start | bytes 1572872 | tf_op jit(solution)/shard_map/ppermute | solution.py:332
  30.0 19.7 %collective-permute-start.5 = (bf16[16,2048]{1,0:T(8,128)(2,1)S(1)}, bf16[16,2048]{1,0:T(8,128)(2,1)S(1)}, u32[]{:S(2)}, u32[]{:S(2)}) collective-permute-start(bf16[16,2048]{1,0:T(8,128)(2,1)S(1)} %get-tuple-element.47.state), channel_id=1, source_target_pairs={{0,8},{8,16},{16,24},{1,9},{9,17},{17,25},{2,10},{10,18},{18,26},{... | collective-permute-start | bytes 196616 | tf_op jit(solution)/shard_map/ppermute | solution.py:332
  34.3 15.4 %collective-permute-start.6 = (bf16[16,2048]{1,0:T(8,128)(2,1)S(1)}, bf16[16,2048]{1,0:T(8,128)(2,1)S(1)}, u32[]{:S(2)}, u32[]{:S(2)}) collective-permute-start(bf16[16,2048]{1,0:T(8,128)(2,1)S(1)} %get-tuple-element.47.state), channel_id=1, source_target_pairs={{0,16},{8,24},{1,17},{9,25},{2,18},{10,26},{3,19},{11,27},{4,20},{... | collective-permute-start | bytes 196616 | tf_op jit(solution)/shard_map/ppermute | solution.py:332
  40.2 9.6 %collective-permute-start.7 = (bf16[16,2048]{1,0:T(8,128)(2,1)S(1)}, bf16[16,2048]{1,0:T(8,128)(2,1)S(1)}, u32[]{:S(2)}, u32[]{:S(2)}) collective-permute-start(bf16[16,2048]{1,0:T(8,128)(2,1)S(1)} %get-tuple-element.47.state), channel_id=1, source_target_pairs={{0,24},{1,25},{2,26},{3,27},{4,28},{5,29},{6,30},{7,31}} | collective-permute-start | bytes 196616 | tf_op jit(solution)/shard_map/ppermute | solution.py:332
  49.8 2.5 %collective-permute-start.8 = (bf16[9,16,128]{2,1,0:T(8,128)(2,1)S(1)}, bf16[9,16,128]{2,1,0:T(8,128)(2,1)S(1)}, u32[]{:S(2)}, u32[]{:S(2)}) collective-permute-start(bf16[9,16,128]{2,1,0:T(8,128)(2,1)S(1)} %sums.1), channel_id=1, source_target_pairs={{0,1},{1,0},{2,3},{3,2},{4,5},{5,4},{6,7},{7,6},{8,9},{9,8},{10,11... | collective-permute-start | bytes 110600 | tf_op jit(solution)/shard_map/ppermute | solution.py:345
  49.9 2.6 %copy-start.5 = (bf16[1,2048,128]{2,1,0:T(8,128)(2,1)S(1)}, bf16[1,2048,128]{2,1,0:T(8,128)(2,1)}, u32[]{:S(2)}) copy-start(bf16[1,2048,128]{2,1,0:T(8,128)(2,1)} %param.9) | copy-start | bytes 1572868
  49.9 2.6 %copy-start.6 = (bf16[1,2048,128]{2,1,0:T(8,128)(2,1)S(1)}, bf16[1,2048,128]{2,1,0:T(8,128)(2,1)}, u32[]{:S(2)}) copy-start(bf16[1,2048,128]{2,1,0:T(8,128)(2,1)} %param.10) | copy-start | bytes 1572868
  52.4 4.4 %collective-permute-start.9 = (bf16[9,16,128]{2,1,0:T(8,128)(2,1)S(1)}, bf16[9,16,128]{2,1,0:T(8,128)(2,1)S(1)}, u32[]{:S(2)}, u32[]{:S(2)}) collective-permute-start(bf16[9,16,128]{2,1,0:T(8,128)(2,1)S(1)} %add_convert_fusion.1), channel_id=1, source_target_pairs={{0,8},{8,0},{16,24},{24,16},{1,9},{9,1},{17,25},{25,17},{2,10},{10... | collective-permute-start | bytes 110600 | tf_op jit(solution)/shard_map/ppermute | solution.py:345
  56.8 4.9 %collective-permute-start.10 = (bf16[9,16,128]{2,1,0:T(8,128)(2,1)S(1)}, bf16[9,16,128]{2,1,0:T(8,128)(2,1)S(1)}, u32[]{:S(2)}, u32[]{:S(2)}) collective-permute-start(bf16[9,16,128]{2,1,0:T(8,128)(2,1)S(1)} %add_convert_fusion.half), channel_id=1, source_target_pairs={{0,16},{8,24},{16,0},{24,8},{1,17},{9,25},{17,1},{25,9},{2,18},{10... | collective-permute-start | bytes 110600 | tf_op jit(solution)/shard_map/ppermute | solution.py:345
where the time goes:
time: 62.7 us; the launch traced here: 62.4 us
  Pallas kernels  33.6 us (54%)
  starting transfers between devices  21.7 us (35%)
  waiting for transfers between devices  6.02 us (10%)
  between operations  0.94 us (1%)
    ppermute x8, starting transfers between devices, shifted(): lax.ppermute(value, axis, [(source, source + steps) for source in range(f...  21.5 us
    pallas_call x1, Pallas kernels, per_device(): call(sums_kernel, 'sums', [wide] * 7 + [narrow, narrow, modes], [whole],...  8.28 us
    pallas_call x1, Pallas kernels, per_device(): call(local_kernel, 'local', [wide, wide, modes, modes], [wide] * 5 + [tab...  5.5 us
    pallas_call x1, Pallas kernels, per_device(): call(forward_kernel, 'forward', [wide, wide, table, wide, wide, wide, wid...  4.98 us
    pallas_call x1, Pallas kernels, per_device(): call(product_kernel, 'product', [wide, wide, table, wide, wide], [wide, w...  4.32 us
    pallas_call x1, Pallas kernels, per_device(): call(first_kernel, 'first', [wide] * 4 + [modes], [wide, narrow], [wide_h...  4.07 us
    ppermute x8, waiting for transfers between devices, shifted(): lax.ppermute(value, axis, [(source, source + steps) for source in range(f...  3.35 us
    ppermute x3, waiting for transfers between devices, exchanged(): other = lax.ppermute(half, axis, pairs)  2.67 us
  transfers between devices with their start and end apart: 11, of which 2 were waited for; matrix products, arithmetic and copies ran while one was open for 0% of the time, Pallas kernels for 46%

commit v1 on v0

--- a/solution.py
+++ b/solution.py
@@ -147,19 +147,42 @@
     return cols == rows // LANES + (at * blocks + block) * PACK
 
 
-def first_kernel(query, key, grad, value, rate, product, state):
+def first_kernel(query, key, grad, value, rate, product, states, held, arrived):
     rows, cols = iotas()
     offsets = cols.astype(F32)
     mask = rows // LANES == cols // LANES
-    at = pl.program_id(0)
-    blocks = product.shape[0] // TILE
-    for block in range(blocks):
-        span = pl.ds(block * TILE, TILE)
-        rates = column(rate[...], block_groups(at, blocks, block))
-        powers = jnp.exp(-rates * offsets).astype(BF16)
-        dz2 = grad[span, :] * value[span, :]
-        state[:, span] = squeeze_groups(nt(powers, dz2), mask).astype(BF16)
-        product[span, :] = query[span, :] * key[span, :]
+    size = held.shape[1] // STEPS
+    blocks = size // TILE
+    streams = (grad, value, query, key)
+
+    def fetch(array, step):
+        span = pl.ds(step * size, size)
+        return pltpu.make_async_copy(
+            streams[array].at[span, :], held.at[array, span, :], arrived.at[array, step]
+        )
+
+    for step in range(STEPS):
+        for array in range(2):
+            fetch(array, step).start()
+    for step in range(STEPS):
+        for array in range(2, 4):
+            fetch(array, step).start()
+    for step in range(STEPS):
+        for array in range(2):
+            fetch(array, step).wait()
+        for block in range(step * blocks, (step + 1) * blocks):
+            span = pl.ds(block * TILE, TILE)
+            rates = column(rate[...], block_groups(0, 0, block))
+            powers = jnp.exp(-rates * offsets).astype(BF16)
+            dz2 = held[0, span, :] * held[1, span, :]
+            state = squeeze_groups(nt(powers, dz2), mask).astype(BF16)
+            for place in range(states.shape[0]):
+                states[place, :, span] = state
+    for step in range(STEPS):
+        for array in range(2, 4):
+            fetch(array, step).wait()
+        span = pl.ds(step * size, size)
+        product[span, :] = held[2, span, :] * held[3, span, :]
 
 
 def local_kernel(grad, value, rate, residue, du2, to_next, after, to_end, power, taps, decay):
@@ -196,17 +219,17 @@
         du2[span, :] = within_shard(dz2, turned[block * PACK : (block + 1) * PACK], lower_half)
 
 
-def middle_kernel(count, *refs):
-    states = refs[: count - 1]
-    local, to_next, decay, li_key, value, dz1, du2, after_shard = refs[count - 1 :]
+def middle_kernel(states, local, to_next, decay, li_key, value, dz1, du2, after_shard):
     rows, cols = iotas()
     mask = rows // LANES == cols // LANES
+    place = lax.axis_index("seq")
     for block in range(local.shape[0] // TILE):
         span = pl.ds(block * TILE, TILE)
         fade = decay[:, span]
-        carried = states[-1][:, span].astype(F32)
-        for state in states[-2::-1]:
-            carried = state[:, span].astype(F32) + fade * carried
+        carried = jnp.zeros((LANES, TILE), F32)
+        for source in range(states.shape[0] - 1, 0, -1):
+            longer = states[source, :, span].astype(F32) + fade * carried
+            carried = jnp.where(place < source, longer, carried)
         after_shard[:, span] = carried
         wide = spread_groups(carried, mask).T.astype(BF16)
         total = local[span, :] + nn(wide, to_next[span, :])
@@ -216,7 +239,7 @@
 
 
 def forward_kernel(
-    before, now, filters, value, li_key, to_end, du2, grad_value, grad_key, u2, state
+    before, now, filters, value, li_key, to_end, du2, grad_value, grad_key, u2, states
 ):
     rows, cols = iotas()
     mask = rows // LANES == cols // LANES
@@ -229,14 +252,16 @@
         key_two = li_key[span, :].astype(F32)
         u2_half = (y1 * key_two).astype(BF16)
         u2[span, :] = u2_half
-        state[:, span] = squeeze_groups(nt(to_end[span, :], u2_half), mask).astype(BF16)
+        state = squeeze_groups(nt(to_end[span, :], u2_half), mask).astype(BF16)
+        for place in range(states.shape[0]):
+            states[place, :, span] = state
         du2_here = du2[span, :]
         grad_key[span, :] = (du2_here * y1).astype(BF16)
         grad_value[span, :] = (du2_here * key_two * z1).astype(BF16)
 
 
 def sums_kernel(
-    before, now, u2, dz1, grad, li_value, power, state, after_shard, rate,
+    before, now, u2, dz1, grad, li_value, power, states, after_shard, rate,
     packed, filter_sums, within_sums, across_sums,
 ):
     rows, cols = iotas()
@@ -268,7 +293,7 @@
         energies = jnp.concatenate([energies] * LANES, axis=0)
         own = block_groups(at, blocks, block)
         within_sums[...] += squeeze_groups(nt(power[span, :], energies), own)
-        across = state[:, span].astype(F32) * after_shard[:, span]
+        across = states[0, :, span].astype(F32) * after_shard[:, span]
         across_sums[...] += nn(across.astype(BF16), ones_where(own))
 
     @pl.when(at == STEPS - 1)
@@ -298,7 +323,8 @@
     grad_residue[...] = half[chunks].astype(F32) + other[chunks].astype(F32)
 
 
-def product_kernel(dz1, later, filters, query, key, grad_query, grad_key):
+def product_kernel(dz1, later, filters, query, key, *refs):
+    grad_query, grad_key = refs[-2:]
     rows, cols = iotas()
     lower_half = ones_where(rows >= cols)
     turned = nn(filters[...], reversal())
@@ -310,17 +336,17 @@
         grad_key[span, :] = (du1 * query[span, :].astype(F32)).astype(BF16)
 
 
-def value_kernel(count, *refs):
-    states = refs[: count - 1]
-    after, decay, z2, grad, grad_value = refs[count - 1 :]
+def value_kernel(states, after, decay, z2, grad, grad_value):
     rows, cols = iotas()
     mask = rows // LANES == cols // LANES
+    place = lax.axis_index("seq")
     for block in range(z2.shape[0] // TILE):
         span = pl.ds(block * TILE, TILE)
         fade = decay[:, span]
-        carried = states[-1][:, span].astype(F32)
-        for state in states[-2::-1]:
-            carried = state[:, span].astype(F32) + fade * carried
+        carried = jnp.zeros((LANES, TILE), F32)
+        for source in range(states.shape[0] - 1):
+            longer = states[source, :, span].astype(F32) + fade * carried
+            carried = jnp.where(place > source, longer, carried)
         wide = spread_groups(carried, mask).T.astype(BF16)
         total = z2[span, :] + nn(wide, after[span, :])
         grad_value[span, :] = (grad[span, :].astype(F32) * total).astype(BF16)
@@ -332,7 +358,11 @@
     return lax.ppermute(value, axis, [(source, source + steps) for source in range(first, last)])
 
 
-def exchanged(half, axes, beside):
+def to_all(states):
+    return lax.all_to_all(states, "seq", 0, 0, tiled=True)
+
+
+def exchanged(half, axes, makers):
     partners = []
     for axis in axes:
         count, bit = lax.axis_size(axis), 1
@@ -343,11 +373,12 @@
     made = []
     for at, (axis, pairs) in enumerate(partners):
         other = lax.ppermute(half, axis, pairs)
+        if at < len(makers):
+            made.append(makers[at](*made[-1:]))
         if at < len(partners) - 1:
             half = (half.astype(F32) + other.astype(F32)).astype(BF16)
-            if at < len(beside):
-                half, arrays = lax.optimization_barrier((half, beside[at]))
-                made.append(arrays)
+            if at < len(makers):
+                half, made[-1] = lax.optimization_barrier((half, made[-1]))
     return half, other, made
 
 
@@ -374,10 +405,12 @@
     modes = pl.BlockSpec((LANES, TILE), lambda i: (0, 0))
     wide_half = jax.ShapeDtypeStruct((channels, TILE), BF16)
     wide_full = jax.ShapeDtypeStruct((channels, TILE), F32)
-    narrow_half = jax.ShapeDtypeStruct((LANES, channels), BF16)
     narrow_full = jax.ShapeDtypeStruct((LANES, channels), F32)
 
-    def call(kernel, name, in_specs, out_specs, out_shape, scratch=(), limit=VMEM_LIMIT, grid=STEPS):
+    copies = pl.BlockSpec((count, LANES, rows), lambda i: (0, 0, i))
+    all_copies = jax.ShapeDtypeStruct((count, LANES, channels), BF16)
+
+    def call(kernel, name, in_specs, out_specs, out_shape, scratch=(), grid=STEPS, work=0, **more):
         return pl.pallas_call(
             kernel,
             grid=(grid,),
@@ -386,71 +419,88 @@
             out_shape=out_shape,
             scratch_shapes=scratch,
             name=name,
-            cost_estimate=pl.CostEstimate(flops=1, bytes_accessed=1, transcendentals=0),
-            compiler_params=pltpu.CompilerParams(vmem_limit_bytes=limit),
+            cost_estimate=pl.CostEstimate(
+                flops=work * 2 * channels * TILE * TILE, bytes_accessed=1, transcendentals=0
+            ),
+            compiler_params=pltpu.CompilerParams(vmem_limit_bytes=more.pop("limit", VMEM_LIMIT)),
+            **more,
         )
 
-    product, back = call(
+    def whole(leaf):
+        return pl.BlockSpec(leaf.shape, lambda i: (0,) * len(leaf.shape))
+
+    product, backs = call(
         first_kernel, "first",
-        [wide] * 4 + [modes], [wide, narrow], [wide_half, narrow_half], limit=60 * 1024 * 1024,
+        [pl.BlockSpec(memory_space=pltpu.HBM)] * 4 + [modes],
+        [whole(wide_half), whole(all_copies)], [wide_half, all_copies],
+        [pltpu.VMEM((4, channels, TILE), BF16), pltpu.SemaphoreType.DMA((4, STEPS))],
+        grid=1, limit=60 * 1024 * 1024,
     )(query, key, grad, value_two, rate)
     product_before = shifted(product, "seq", 1)
-    later_backs = [shifted(back, "seq", -gap) for gap in range(1, count)]
+    all_backs = to_all(backs)
 
     du2_local, to_next, after, to_end, power, taps, decay = call(
         local_kernel, "local",
         [wide, wide, modes, modes],
         [wide] * 5 + [table, narrow],
         [wide_full] + [wide_half] * 4 + [jax.ShapeDtypeStruct((groups, TILE), F32), narrow_full],
+        work=20,
     )(grad, value_two, rate, residue)
 
     dz1, du2, after_shard = call(
-        functools.partial(middle_kernel, count), "middle",
-        [narrow] * (count - 1) + [wide, wide, narrow, wide, wide],
+        middle_kernel, "middle",
+        [copies, wide, wide, narrow, wide, wide],
         [wide, wide, narrow], [wide_half, wide_full, narrow_full],
-    )(*later_backs, du2_local, to_next, decay, key_two, value)
-    dz1_later = shifted(dz1, "seq", -1)
-
-    grad_mr_value, grad_li_key, u2, state = call(
+    )(all_backs, du2_local, to_next, decay, key_two, value)
+
+    grad_mr_value, grad_li_key, u2, states = call(
         forward_kernel, "forward",
         [wide, wide, table, wide, wide, wide, wide],
-        [wide, wide, wide, narrow], [wide_half] * 3 + [narrow_half],
+        [wide, wide, wide, copies], [wide_half] * 3 + [all_copies],
     )(product_before, product, mr_filter, value, key_two, to_end, du2)
-    earlier_states = [shifted(state, "seq", gap) for gap in range(1, count)]
-
-    chunks = groups // LANES + 1
-    whole = pl.BlockSpec((chunks, LANES, TILE), lambda i: (0, 0, 0))
+    all_states = to_all(states)
+
+    (z2,) = call(within_kernel, "within", [wide, table], [wide], [wide_full])(u2, taps)
+
+    dz1_sent, u2_kept, z2, all_states = lax.optimization_barrier((dz1, u2, z2, all_states))
+    dz1_later = shifted(dz1_sent, "seq", -1)
+
+    sums_shape = jax.ShapeDtypeStruct((groups // LANES + 1, LANES, TILE), BF16)
     (packed,) = call(
         sums_kernel, "sums",
-        [wide] * 7 + [narrow, narrow, modes],
-        [whole], [jax.ShapeDtypeStruct((chunks, LANES, TILE), BF16)],
+        [wide] * 7 + [copies, narrow, modes],
+        [whole(sums_shape)], [sums_shape],
         [pltpu.VMEM((groups, TILE), F32)] + [pltpu.VMEM((LANES, TILE), F32)] * 2,
-    )(product_before, product, u2, dz1, grad, value_two, power, state, after_shard, rate)
-    packed, dz1_later, *earlier_states = lax.optimization_barrier(
-        (packed, dz1_later, *earlier_states)
+    )(product_before, product, u2_kept, dz1, grad, value_two, power, states, after_shard, rate)
+    all_states, dz1_later = lax.optimization_barrier((all_states, dz1_later))
+
+    def make_value():
+        return call(
+            value_kernel, "value", [copies, wide, narrow, wide, wide], [wide], [wide_half]
+        )(all_states, after, decay, z2, grad)
+
+    def make_products(part, *halves):
+        def blocks(spec):
+            return pl.BlockSpec(spec.block_shape, lambda i: (i + part * (STEPS // 2), 0))
+
+        kept = [pl.BlockSpec(memory_space=pl.ANY)] * len(halves)
+        return call(
+            product_kernel, "product",
+            [blocks(spec) for spec in (wide, wide, table, wide, wide)] + kept,
+            [blocks(wide)] * 2, [wide_half, wide_half], grid=STEPS // 2,
+            input_output_aliases={5 + at: at for at in range(len(halves))},
+        )(dz1, dz1_later, mr_filter, query, key, *halves)
+
+    half, other, ((grad_li_value,), _, (grad_query, grad_key)) = exchanged(
+        packed, ("dp", "seq"),
+        [lambda: make_value(), lambda _: make_products(0), lambda halves: make_products(1, *halves)],
     )
 
-    (z2,) = call(within_kernel, "within", [wide, table], [wide], [wide_full])(u2, taps)
-
-    products = call(
-        product_kernel, "product",
-        [wide, wide, table, wide, wide], [wide, wide], [wide_half, wide_half],
-    )(dz1, dz1_later, mr_filter, query, key)
-
-    half, other, ((z2,), (grad_query, grad_key)) = exchanged(
-        packed, ("dp", "seq"), [[z2], products]
-    )
-
-    (grad_li_value,) = call(
-        functools.partial(value_kernel, count), "value",
-        [narrow] * (count - 1) + [wide, narrow, wide, wide], [wide], [wide_half],
-    )(*earlier_states, after, decay, z2, grad)
-
-    all_groups = pl.BlockSpec((groups, TILE), lambda i: (0, 0))
+    filter_shape = jax.ShapeDtypeStruct((groups, TILE), F32)
+    residue_shape = jax.ShapeDtypeStruct((LANES, TILE), F32)
     grad_filter, grad_residue = call(
-        last_kernel, "last", [whole, whole], [all_groups, modes],
-        [jax.ShapeDtypeStruct((groups, TILE), F32), jax.ShapeDtypeStruct((LANES, TILE), F32)],
-        grid=1,
+        last_kernel, "last", [whole(sums_shape)] * 2,
+        [whole(filter_shape), whole(residue_shape)], [filter_shape, residue_shape], grid=1,
     )(half, other)
     return (
         grad_query[None],

time: 62.7 us -> 79.3 us (1.26)
  local copies, waits for them, and re-layouts: 0.05 us -> 13.8 us
  Pallas kernels: 33.6 us -> 35.2 us
  waiting for transfers between devices: 6.02 us -> 7.37 us
    ppermute x8 -> x2, starting transfers between devices: 21.5 us -> 6.37 us  [shifted(): lax.ppermute(value, axis, [(source, source + steps) for source in range(f...]
    unnamed x20 -> x58, local copies, waits for them, and re-layouts: 0.05 us -> 13.8 us
    all_to_all x0 -> x2, starting transfers between devices: none -> 10.8 us  [to_all(): return lax.all_to_all(states, 'seq', 0, 0, tiled=True)]
    all_to_all x0 -> x2, waiting for transfers between devices: none -> 5.11 us  [to_all(): return lax.all_to_all(states, 'seq', 0, 0, tiled=True)]
    ppermute x3, starting transfers between devices: 0.21 us -> 4.09 us  [exchanged(): other = lax.ppermute(half, axis, pairs)]
    ppermute x8 -> x2, waiting for transfers between devices: 3.35 us -> 0.01 us  [shifted(): lax.ppermute(value, axis, [(source, source + steps) for source in range(f...]
    pallas_call x6 -> x7, Pallas kernels: 20.7 us -> 22.2 us  [the longest x1 9.18 us: per_device(): call(sums_kernel, 'sums', [wide] * 7 + [copies, narrow, modes], [whole(su...]
  transfers between devices with their start and end apart: 11 -> 7, of which waited for: 2 -> 4; matrix products, arithmetic and copies ran while one was open for 0% -> 0% of each run, Pallas kernels for 46% -> 30%
where the time goes in v1:
time: 79.3 us; the launch traced here: 78.5 us
  Pallas kernels  35.2 us (44%)
  starting transfers between devices  21.2 us (27%)
  local copies, waits for them, and re-layouts  13.8 us (17%)
  waiting for transfers between devices  7.37 us (9%)
  between operations  0.86 us (1%)
    unnamed x58, local copies, waits for them, and re-layouts  13.8 us
    all_to_all x2, starting transfers between devices, to_all(): return lax.all_to_all(states, 'seq', 0, 0, tiled=True)  10.8 us
    pallas_call x1, Pallas kernels, per_device(): call(sums_kernel, 'sums', [wide] * 7 + [copies, narrow, modes], [whole(su...  9.18 us
    ppermute x2, starting transfers between devices, shifted(): lax.ppermute(value, axis, [(source, source + steps) for source in range(f...  6.37 us
    pallas_call x1, Pallas kernels, per_device(): call(local_kernel, 'local', [wide, wide, modes, modes], [wide] * 5 + [tab...  5.51 us
    pallas_call x1, Pallas kernels, per_device(): call(forward_kernel, 'forward', [wide, wide, table, wide, wide, wide, wid...  5.11 us
    all_to_all x2, waiting for transfers between devices, to_all(): return lax.all_to_all(states, 'seq', 0, 0, tiled=True)  5.11 us
    pallas_call x2, Pallas kernels, make_products(): call(product_kernel, 'product', [blocks(spec) for spec in (wide, wide, ta...  5.01 us
  transfers between devices with their start and end apart: 7, of which 4 were waited for; matrix products, arithmetic and copies ran while one was open for 0% of the time, Pallas kernels for 30%

profile of v1, /device:TPU:0, one launch (start us, length us, event | category | flops | bytes accessed | tf_op | source)
XLA Modules:
  0.0 78.5 jit_solution(12774665693825006257)
XLA Ops:
  0.6 0.0 copy-start.9
  0.6 0.0 copy-start.27
  0.7 4.0 %first.1 = (bf16[2048,128]{1,0:T(8,128)(2,1)}, bf16[4,16,2048]{2,1,0:T(8,128)(2,1)}) custom-call(bf16[2048,128]{1,0:T(8,128)(2,1)} %bitcast.18, bf16[2048,128]{1,0:T(8,128)(2,1)} %bitcast.21, bf16[2048,128]{1,0:T(8,128)(2,1)} %bitcast.14, bf16[2048,128]{1,0:T(8,128)(2,1)} %bitcast.28, f32[16,128]{1,0:T(8,128)} %bitcast.31), custom_call_target="tpu_custom_call" | custom-call | bytes 1 | tf_op jit(solution)/shard_map/first/pallas_call | solution.py:432
  4.6 0.0 copy-start
  4.6 5.1 %collective-permute-start = (bf16[2048,128]{1,0:T(8,128)(2,1)}, bf16[2048,128]{1,0:T(8,128)(2,1)S(1)}, u32[]{:S(2)}, u32[]{:S(2)}) collective-permute-start(bf16[2048,128]{1,0:T(8,128)(2,1)} %get-tuple-element.45.now), channel_id=1, source_target_pairs={{0,8},{8,16},{16,24},{1,9},{9,17},{17,25},{2,10},{10,18},{18,26},{... | collective-permute-start | bytes 1572872 | tf_op jit(solution)/shard_map/ppermute | solution.py:358
  9.7 3.8 %all-to-all-start = ((bf16[4,16,2048]{2,1,0:T(8,128)(2,1)}), bf16[4,16,2048]{2,1,0:T(8,128)(2,1)S(1)}, u32[]{:S(2)}, u32[]{:S(2)}) async-start(bf16[4,16,2048]{2,1,0:T(8,128)(2,1)} %get-tuple-element.40), calls=%async_computation | async-start | bytes 524288 | tf_op jit(solution)/shard_map/all_to_all | solution.py:362
  13.6 0.0 copy-start.7
  13.6 0.0 copy-start.8
  13.6 5.5 %local.1 = (f32[2048,128]{1,0:T(8,128)S(1)}, bf16[2048,128]{1,0:T(8,128)(2,1)S(1)}, bf16[2048,128]{1,0:T(8,128)(2,1)S(1)}, bf16[2048,128]{1,0:T(8,128)(2,1)S(1)}...) custom-call(bf16[2048,128]{1,0:T(8,128)(2,1)S(1)} %bitcast.15, ...), custom_call_target="tpu_custom_call" | custom-call | flops 1342177280 | bytes 1 | tf_op jit(solution)/shard_map/local/pallas_call | solution.py:442
  19.1 1.0 %copy-done.11 = f32[2048,128]{1,0:T(8,128)} copy-done((f32[2048,128]{1,0:T(8,128)}, f32[2048,128]{1,0:T(8,128)S(1)}, u32[]{:S(2)}) %copy-start.11) | copy-done | bytes 1048600
  20.1 0.8 %copy-done.13 = bf16[2048,128]{1,0:T(8,128)(2,1)} copy-done((bf16[2048,128]{1,0:T(8,128)(2,1)}, bf16[2048,128]{1,0:T(8,128)(2,1)S(1)}, u32[]{:S(2)}) %copy-start.13) | copy-done | bytes 524312
  20.9 0.8 %copy-done.15 = bf16[2048,128]{1,0:T(8,128)(2,1)} copy-done((bf16[2048,128]{1,0:T(8,128)(2,1)}, bf16[2048,128]{1,0:T(8,128)(2,1)S(1)}, u32[]{:S(2)}) %copy-start.15) | copy-done | bytes 524312
  21.7 0.8 %copy-done.17 = bf16[2048,128]{1,0:T(8,128)(2,1)} copy-done((bf16[2048,128]{1,0:T(8,128)(2,1)}, bf16[2048,128]{1,0:T(8,128)(2,1)S(1)}, u32[]{:S(2)}) %copy-start.17) | copy-done | bytes 524312
  22.5 0.8 %copy-done.19 = bf16[2048,128]{1,0:T(8,128)(2,1)} copy-done((bf16[2048,128]{1,0:T(8,128)(2,1)}, bf16[2048,128]{1,0:T(8,128)(2,1)S(1)}, u32[]{:S(2)}) %copy-start.19) | copy-done | bytes 524312
  23.3 0.6 copy-done.25
  23.9 1.5 %all-to-all-done.states = bf16[4,16,2048]{2,1,0:T(8,128)(2,1)S(1)} async-done(((bf16[4,16,2048]{2,1,0:T(8,128)(2,1)}), bf16[4,16,2048]{2,1,0:T(8,128)(2,1)S(1)}, u32[]{:S(2)}, u32[]{:S(2)}) %all-to-all-start) | async-done | bytes 262176 | tf_op jit(solution)/shard_map/all_to_all | solution.py:362
  25.5 1.2 %copy-done.12 = f32[2048,128]{1,0:T(8,128)S(1)} copy-done((f32[2048,128]{1,0:T(8,128)S(1)}, f32[2048,128]{1,0:T(8,128)}, u32[]{:S(2)}) %copy-start.12) | copy-done | bytes 1048600
  26.7 1.0 %copy-done.20 = bf16[2048,128]{1,0:T(8,128)(2,1)S(1)} copy-done((bf16[2048,128]{1,0:T(8,128)(2,1)S(1)}, bf16[2048,128]{1,0:T(8,128)(2,1)}, u32[]{:S(2)}) %copy-start.20) | copy-done | bytes 524312
  27.7 1.2 %middle.1 = (bf16[2048,128]{1,0:T(8,128)(2,1)S(1)}, f32[2048,128]{1,0:T(8,128)S(1)}, f32[16,2048]{1,0:T(8,128)S(1)}) custom-call(bf16[4,16,2048]{2,1,0:T(8,128)(2,1)S(1)} %all-to-all-done.states, f32[2048,128]{1,0:T(8,128)S(1)} %copy-done.12, bf16[2048,128]{1,0:T(8,128)(2,1)S(1)} %copy-done.20, f32[16,2048]{1,0:T(8,128)S(1)} %get-tuple-element.43.decay, ...), custom_call_target="tpu_custom_call" | custom-call | bytes 1 | tf_op jit(solution)/shard_map/middle/pallas_call | solution.py:450
  29.0 0.0 collective-permute-done.before
  29.0 5.1 %forward.1 = (bf16[2048,128]{1,0:T(8,128)(2,1)}, bf16[2048,128]{1,0:T(8,128)(2,1)}, bf16[2048,128]{1,0:T(8,128)(2,1)S(1)}, bf16[4,16,2048]{2,1,0:T(8,128)(2,1)}) custom-call(bf16[2048,128]{1,0:T(8,128)(2,1)S(1)} %collective-permute-done.before, bf16[2048,128]{1,0:T(8,128)(2,1)S(1)} %copy-done.3, bf16[128,128]{1,0:T(8,128)(2,1)S(1)} %copy-done.21, ...), custom_call_target="tpu_custom_call" | custom-call | bytes 1 | tf_op jit(solution)/shard_map/forward/pallas_call | solution.py:456
  34.1 0.8 %copy-done.4 = bf16[2048,128]{1,0:T(8,128)(2,1)} copy-done((bf16[2048,128]{1,0:T(8,128)(2,1)}, bf16[2048,128]{1,0:T(8,128)(2,1)S(1)}, u32[]{:S(2)}) %copy-start.4) | copy-done | bytes 524312
  34.9 6.9 %all-to-all-start.1 = ((bf16[4,16,2048]{2,1,0:T(8,128)(2,1)}), bf16[4,16,2048]{2,1,0:T(8,128)(2,1)S(1)}, u32[]{:S(2)}, u32[]{:S(2)}) async-start(bf16[4,16,2048]{2,1,0:T(8,128)(2,1)} %get-tuple-element.50.states), calls=%async_computation.1 | async-start | bytes 524288 | tf_op jit(solution)/shard_map/all_to_all | solution.py:362
  41.8 1.0 %copy-done.5 = bf16[2048,128]{1,0:T(8,128)(2,1)S(1)} copy-done((bf16[2048,128]{1,0:T(8,128)(2,1)S(1)}, bf16[2048,128]{1,0:T(8,128)(2,1)}, u32[]{:S(2)}) %copy-start.5) | copy-done | bytes 524312
  42.9 0.8 %copy-done.26 = f32[128,128]{1,0:T(8,128)S(1)} copy-done((f32[128,128]{1,0:T(8,128)S(1)}, f32[128,128]{1,0:T(8,128)}, u32[]{:S(2)}) %copy-start.26) | copy-done | bytes 65560
  43.7 2.4 %within.1.z2 = f32[2048,128]{1,0:T(8,128)S(1)} custom-call(bf16[2048,128]{1,0:T(8,128)(2,1)S(1)} %copy-done.5, f32[128,128]{1,0:T(8,128)S(1)} %copy-done.26), custom_call_target="tpu_custom_call" | custom-call | bytes 1 | tf_op jit(solution)/shard_map/within/pallas_call | solution.py:463
  46.1 3.6 %all-to-all-done.1.states = bf16[4,16,2048]{2,1,0:T(8,128)(2,1)S(1)} async-done(((bf16[4,16,2048]{2,1,0:T(8,128)(2,1)}), bf16[4,16,2048]{2,1,0:T(8,128)(2,1)S(1)}, u32[]{:S(2)}, u32[]{:S(2)}) %all-to-all-start.1) | async-done | bytes 262176 | tf_op jit(solution)/shard_map/all_to_all | solution.py:362
  49.7 1.3 %collective-permute-start.1 = (bf16[2048,128]{1,0:T(8,128)(2,1)S(1)}, bf16[2048,128]{1,0:T(8,128)(2,1)S(1)}, u32[]{:S(2)}, u32[]{:S(2)}) collective-permute-start(bf16[2048,128]{1,0:T(8,128)(2,1)S(1)} %get-tuple-element.52.dz1), channel_id=1, source_target_pairs={{8,0},{16,8},{24,16},{9,1},{17,9},{25,17},{10,2},{18,10},{26,18},{... | collective-permute-start | bytes 1572872 | tf_op jit(solution)/shard_map/ppermute | solution.py:358
  51.0 0.0 copy-start.6
  51.0 1.0 %copy-done.6 = bf16[2048,128]{1,0:T(8,128)(2,1)S(1)} copy-done((bf16[2048,128]{1,0:T(8,128)(2,1)S(1)}, bf16[2048,128]{1,0:T(8,128)(2,1)}, u32[]{:S(2)}) %copy-start.6) | copy-done | bytes 524312
  52.1 1.0 %copy-done.10 = bf16[1,2048,128]{2,1,0:T(8,128)(2,1)S(1)} copy-done((bf16[1,2048,128]{2,1,0:T(8,128)(2,1)S(1)}, bf16[1,2048,128]{2,1,0:T(8,128)(2,1)}, u32[]{:S(2)}) %copy-start.10) | copy-done | bytes 524312
  53.1 1.0 %copy-done.14 = bf16[2048,128]{1,0:T(8,128)(2,1)S(1)} copy-done((bf16[2048,128]{1,0:T(8,128)(2,1)S(1)}, bf16[2048,128]{1,0:T(8,128)(2,1)}, u32[]{:S(2)}) %copy-start.14) | copy-done | bytes 524312
  54.1 0.9 %copy-done.24 = f32[16,2048]{1,0:T(8,128)S(1)} copy-done((f32[16,2048]{1,0:T(8,128)S(1)}, f32[16,2048]{1,0:T(8,128)}, u32[]{:S(2)}) %copy-start.24) | copy-done | bytes 131096
  55.0 9.2 %sums.1 = bf16[9,16,128]{2,1,0:T(8,128)(2,1)S(1)} custom-call(bf16[2048,128]{1,0:T(8,128)(2,1)S(1)} %collective-permute-done.before, bf16[2048,128]{1,0:T(8,128)(2,1)S(1)} %copy-done.3, bf16[2048,128]{1,0:T(8,128)(2,1)S(1)} %copy-done.6, bf16[2048,128]{1,0:T(8,128)(2,1)S(1)} %get-tuple-element.52.dz1, bf16[2048,128]{1,0:T(8,128)(2,1)S(1)} %bitcast.16, ...), custom_call_target="tpu_custom_call" | custom-call | bytes 1 | tf_op jit(solution)/shard_map/sums/pallas_call | solution.py:469
  64.2 0.1 collective-permute-start.2
  64.3 1.2 %collective-permute-done.2 = bf16[9,16,128]{2,1,0:T(8,128)(2,1)S(1)} collective-permute-done((bf16[9,16,128]{2,1,0:T(8,128)(2,1)S(1)}, bf16[9,16,128]{2,1,0:T(8,128)(2,1)S(1)}, u32[]{:S(2)}, u32[]{:S(2)}) %collective-permute-start.2) | collective-permute-done | bytes 36896 | tf_op jit(solution)/shard_map/ppermute | solution.py:375
  65.5 0.0 collective-permute-done.1.later
  65.6 0.0 copy-start.1
  65.6 0.0 copy-start.2
  65.6 0.0 copy-start.22
  65.6 2.2 %value.1 = bf16[2048,128]{1,0:T(8,128)(2,1)} custom-call(bf16[4,16,2048]{2,1,0:T(8,128)(2,1)S(1)} %all-to-all-done.1.states, bf16[2048,128]{1,0:T(8,128)(2,1)S(1)} %copy-done.18, f32[16,2048]{1,0:T(8,128)S(1)} %get-tuple-element.43.decay, f32[2048,128]{1,0:T(8,128)S(1)} %within.1.z2, bf16[2048,128]{1,0:T(8,128)(2,1)S(1)} %bitcast.17), custom_call_target="tpu_custom_call" | custom-call | bytes 1 | tf_op jit(solution)/shard_map/value/pallas_call | solution.py:478
  67.8 2.6 %collective-permute-start.3 = (bf16[9,16,128]{2,1,0:T(8,128)(2,1)S(1)}, bf16[9,16,128]{2,1,0:T(8,128)(2,1)S(1)}, u32[]{:S(2)}, u32[]{:S(2)}) collective-permute-start(bf16[9,16,128]{2,1,0:T(8,128)(2,1)S(1)} %add_convert_fusion.1), channel_id=1, source_target_pairs={{0,8},{8,0},{16,24},{24,16},{1,9},{9,1},{17,25},{25,17},{2,10},{10... | collective-permute-start | bytes 110600 | tf_op jit(solution)/shard_map/ppermute | solution.py:375
  70.4 2.5 %product.2 = (bf16[2048,128]{1,0:T(8,128)(2,1)}, bf16[2048,128]{1,0:T(8,128)(2,1)}) custom-call(bf16[2048,128]{1,0:T(8,128)(2,1)S(1)} %get-tuple-element.52.dz1, bf16[2048,128]{1,0:T(8,128)(2,1)S(1)} %collective-permute-done.1.later, bf16[128,128]{1,0:T(8,128)(2,1)S(1)} %copy-done.22, bf16[2048,128]{1,0:T(8,128)(2,1)S(1)} %bitcast.19, ...), custom_call_target="tpu_custom_call" | custom-call | bytes 1 | tf_op jit(solution)/shard_map/product/pallas_call | solution.py:487
  73.0 0.0 collective-permute-done.3
  73.0 1.4 %collective-permute-start.4 = (bf16[9,16,128]{2,1,0:T(8,128)(2,1)S(1)}, bf16[9,16,128]{2,1,0:T(8,128)(2,1)S(1)}, u32[]{:S(2)}, u32[]{:S(2)}) collective-permute-start(bf16[9,16,128]{2,1,0:T(8,128)(2,1)S(1)} %add_convert_fusion.half), channel_id=1, source_target_pairs={{0,16},{8,24},{16,0},{24,8},{1,17},{9,25},{17,1},{25,9},{2,18},{10... | collective-permute-start | bytes 110600 | tf_op jit(solution)/shard_map/ppermute | solution.py:375
  74.3 2.5 %product.3 = (bf16[2048,128]{1,0:T(8,128)(2,1)}, bf16[2048,128]{1,0:T(8,128)(2,1)}) custom-call(bf16[2048,128]{1,0:T(8,128)(2,1)S(1)} %get-tuple-element.52.dz1, bf16[2048,128]{1,0:T(8,128)(2,1)S(1)} %collective-permute-done.1.later, bf16[128,128]{1,0:T(8,128)(2,1)S(1)} %copy-done.22, ...), custom_call_target="tpu_custom_call", output_to_operand_aliasing={{0}: (5, {}), {1}: (6, {})} | custom-call | bytes 1 | tf_op jit(solution)/shard_map/product/pallas_call | solution.py:487
  76.8 1.1 %collective-permute-done.4.other = bf16[9,16,128]{2,1,0:T(8,128)(2,1)S(1)} collective-permute-done((bf16[9,16,128]{2,1,0:T(8,128)(2,1)S(1)}, bf16[9,16,128]{2,1,0:T(8,128)(2,1)S(1)}, u32[]{:S(2)}, u32[]{:S(2)}) %collective-permute-start.4) | collective-permute-done | bytes 36896 | tf_op jit(solution)/shard_map/ppermute | solution.py:375
  77.9 0.6 last.1
  (36 shorter events, 0.1 us)
Async XLA Ops:
  0.6 13.0 %copy-start.9 = (bf16[1,2048,128]{2,1,0:T(8,128)(2,1)S(1)}, bf16[1,2048,128]{2,1,0:T(8,128)(2,1)}, u32[]{:S(2)}) copy-start(bf16[1,2048,128]{2,1,0:T(8,128)(2,1)} %param.13) | copy-start | bytes 1572868
  0.6 13.0 %copy-start.27 = (f32[128,16]{0,1:T(8,128)S(1)}, f32[128,16]{0,1:T(8,128)}, u32[]{:S(2)}) copy-start(f32[128,16]{0,1:T(8,128)} %param.17) | copy-start | bytes 24580
  0.7 12.9 %copy-start.28 = (f32[128,16]{0,1:T(8,128)S(1)}, f32[128,16]{0,1:T(8,128)}, u32[]{:S(2)}) copy-start(f32[128,16]{0,1:T(8,128)} %param.16) | copy-start | bytes 24580
  4.6 9.0 %copy-start = (bf16[1,2048,128]{2,1,0:T(8,128)(2,1)S(1)}, bf16[1,2048,128]{2,1,0:T(8,128)(2,1)}, u32[]{:S(2)}) copy-start(bf16[1,2048,128]{2,1,0:T(8,128)(2,1)} %param.14) | copy-start | bytes 1572868
  4.6 24.3 %collective-permute-start = (bf16[2048,128]{1,0:T(8,128)(2,1)}, bf16[2048,128]{1,0:T(8,128)(2,1)S(1)}, u32[]{:S(2)}, u32[]{:S(2)}) collective-permute-start(bf16[2048,128]{1,0:T(8,128)(2,1)} %get-tuple-element.45.now), channel_id=1, source_target_pairs={{0,8},{8,16},{16,24},{1,9},{9,17},{17,25},{2,10},{10,18},{18,26},{... | collective-permute-start | bytes 1572872 | tf_op jit(solution)/shard_map/ppermute | solution.py:358
  9.7 15.7 %all-to-all-start = ((bf16[4,16,2048]{2,1,0:T(8,128)(2,1)}), bf16[4,16,2048]{2,1,0:T(8,128)(2,1)S(1)}, u32[]{:S(2)}, u32[]{:S(2)}) async-start(bf16[4,16,2048]{2,1,0:T(8,128)(2,1)} %get-tuple-element.40), calls=%async_computation | async-start | bytes 524288 | tf_op jit(solution)/shard_map/all_to_all | solution.py:362
  13.6 11.8 %copy-start.7 = (bf16[1,2048,128]{2,1,0:T(8,128)(2,1)S(1)}, bf16[1,2048,128]{2,1,0:T(8,128)(2,1)}, u32[]{:S(2)}) copy-start(bf16[1,2048,128]{2,1,0:T(8,128)(2,1)} %param.12) | copy-start | bytes 1572868
  13.6 11.8 %copy-start.8 = (bf16[1,2048,128]{2,1,0:T(8,128)(2,1)S(1)}, bf16[1,2048,128]{2,1,0:T(8,128)(2,1)}, u32[]{:S(2)}) copy-start(bf16[1,2048,128]{2,1,0:T(8,128)(2,1)} %param.11) | copy-start | bytes 1572868
  19.1 1.0 %copy-start.11 = (f32[2048,128]{1,0:T(8,128)}, f32[2048,128]{1,0:T(8,128)S(1)}, u32[]{:S(2)}) copy-start(f32[2048,128]{1,0:T(8,128)S(1)} %get-tuple-element.41.local) | copy-start | bytes 3145732
  20.1 0.8 %copy-start.13 = (bf16[2048,128]{1,0:T(8,128)(2,1)}, bf16[2048,128]{1,0:T(8,128)(2,1)S(1)}, u32[]{:S(2)}) copy-start(bf16[2048,128]{1,0:T(8,128)(2,1)S(1)} %get-tuple-element.55.power) | copy-start | bytes 1572868
  20.9 0.8 %copy-start.15 = (bf16[2048,128]{1,0:T(8,128)(2,1)}, bf16[2048,128]{1,0:T(8,128)(2,1)S(1)}, u32[]{:S(2)}) copy-start(bf16[2048,128]{1,0:T(8,128)(2,1)S(1)} %get-tuple-element.46.to_end) | copy-start | bytes 1572868
  21.7 0.8 %copy-start.17 = (bf16[2048,128]{1,0:T(8,128)(2,1)}, bf16[2048,128]{1,0:T(8,128)(2,1)S(1)}, u32[]{:S(2)}) copy-start(bf16[2048,128]{1,0:T(8,128)(2,1)S(1)} %get-tuple-element.58.after) | copy-start | bytes 1572868
  22.5 0.8 %copy-start.19 = (bf16[2048,128]{1,0:T(8,128)(2,1)}, bf16[2048,128]{1,0:T(8,128)(2,1)S(1)}, u32[]{:S(2)}) copy-start(bf16[2048,128]{1,0:T(8,128)(2,1)S(1)} %get-tuple-element.42.to_next) | copy-start | bytes 1572868
  23.3 0.6 copy-start.25
  25.5 1.2 %copy-start.12 = (f32[2048,128]{1,0:T(8,128)S(1)}, f32[2048,128]{1,0:T(8,128)}, u32[]{:S(2)}) copy-start(f32[2048,128]{1,0:T(8,128)} %copy-done.11) | copy-start | bytes 3145732
  26.7 1.0 %copy-start.20 = (bf16[2048,128]{1,0:T(8,128)(2,1)S(1)}, bf16[2048,128]{1,0:T(8,128)(2,1)}, u32[]{:S(2)}) copy-start(bf16[2048,128]{1,0:T(8,128)(2,1)} %copy-done.19) | copy-start | bytes 1572868
  27.7 1.2 %copy-start.3 = (bf16[2048,128]{1,0:T(8,128)(2,1)S(1)}, bf16[2048,128]{1,0:T(8,128)(2,1)}, u32[]{:S(2)}) copy-start(bf16[2048,128]{1,0:T(8,128)(2,1)} %get-tuple-element.45.now) | copy-start | bytes 1572868
  27.7 1.2 %copy-start.16 = (bf16[2048,128]{1,0:T(8,128)(2,1)S(1)}, bf16[2048,128]{1,0:T(8,128)(2,1)}, u32[]{:S(2)}) copy-start(bf16[2048,128]{1,0:T(8,128)(2,1)} %copy-done.15) | copy-start | bytes 1572868
  27.7 1.3 %copy-start.21 = (bf16[128,128]{1,0:T(8,128)(2,1)S(1)}, bf16[128,128]{1,0:T(8,128)(2,1)}, u32[]{:S(2)}) copy-start(bf16[128,128]{1,0:T(8,128)(2,1)} %filters.5) | copy-start | bytes 98308
  28.9 5.2 %copy-start.23 = (f32[16,2048]{1,0:T(8,128)}, f32[16,2048]{1,0:T(8,128)S(1)}, u32[]{:S(2)}) copy-start(f32[16,2048]{1,0:T(8,128)S(1)} %get-tuple-element.56.after_shard) | copy-start | bytes 393220
  34.1 0.8 %copy-start.4 = (bf16[2048,128]{1,0:T(8,128)(2,1)}, bf16[2048,128]{1,0:T(8,128)(2,1)S(1)}, u32[]{:S(2)}) copy-start(bf16[2048,128]{1,0:T(8,128)(2,1)S(1)} %get-tuple-element.54.u2) | copy-start | bytes 1572868
  34.9 14.8 %all-to-all-start.1 = ((bf16[4,16,2048]{2,1,0:T(8,128)(2,1)}), bf16[4,16,2048]{2,1,0:T(8,128)(2,1)S(1)}, u32[]{:S(2)}, u32[]{:S(2)}) async-start(bf16[4,16,2048]{2,1,0:T(8,128)(2,1)} %get-tuple-element.50.states), calls=%async_computation.1 | async-start | bytes 524288 | tf_op jit(solution)/shard_map/all_to_all | solution.py:362
  41.8 1.0 %copy-start.5 = (bf16[2048,128]{1,0:T(8,128)(2,1)S(1)}, bf16[2048,128]{1,0:T(8,128)(2,1)}, u32[]{:S(2)}) copy-start(bf16[2048,128]{1,0:T(8,128)(2,1)} %copy-done.4) | copy-start | bytes 1572868
  42.9 0.8 %copy-start.26 = (f32[128,128]{1,0:T(8,128)S(1)}, f32[128,128]{1,0:T(8,128)}, u32[]{:S(2)}) copy-start(f32[128,128]{1,0:T(8,128)} %copy-done.25) | copy-start | bytes 196612
  49.7 15.8 %collective-permute-start.1 = (bf16[2048,128]{1,0:T(8,128)(2,1)S(1)}, bf16[2048,128]{1,0:T(8,128)(2,1)S(1)}, u32[]{:S(2)}, u32[]{:S(2)}) collective-permute-start(bf16[2048,128]{1,0:T(8,128)(2,1)S(1)} %get-tuple-element.52.dz1), channel_id=1, source_target_pairs={{8,0},{16,8},{24,16},{9,1},{17,9},{25,17},{10,2},{18,10},{26,18},{... | collective-permute-start | bytes 1572872 | tf_op jit(solution)/shard_map/ppermute | solution.py:358
  51.0 1.0 %copy-start.6 = (bf16[2048,128]{1,0:T(8,128)(2,1)S(1)}, bf16[2048,128]{1,0:T(8,128)(2,1)}, u32[]{:S(2)}) copy-start(bf16[2048,128]{1,0:T(8,128)(2,1)} %copy-done.4) | copy-start | bytes 1572868
  52.0 1.0 %copy-start.10 = (bf16[1,2048,128]{2,1,0:T(8,128)(2,1)S(1)}, bf16[1,2048,128]{2,1,0:T(8,128)(2,1)}, u32[]{:S(2)}) copy-start(bf16[1,2048,128]{2,1,0:T(8,128)(2,1)} %param.13) | copy-start | bytes 1572868
  53.1 1.0 %copy-start.14 = (bf16[2048,128]{1,0:T(8,128)(2,1)S(1)}, bf16[2048,128]{1,0:T(8,128)(2,1)}, u32[]{:S(2)}) copy-start(bf16[2048,128]{1,0:T(8,128)(2,1)} %copy-done.13) | copy-start | bytes 1572868
  54.1 0.9 %copy-start.24 = (f32[16,2048]{1,0:T(8,128)S(1)}, f32[16,2048]{1,0:T(8,128)}, u32[]{:S(2)}) copy-start(f32[16,2048]{1,0:T(8,128)} %copy-done.23) | copy-start | bytes 393220
  55.0 10.5 %copy-start.18 = (bf16[2048,128]{1,0:T(8,128)(2,1)S(1)}, bf16[2048,128]{1,0:T(8,128)(2,1)}, u32[]{:S(2)}) copy-start(bf16[2048,128]{1,0:T(8,128)(2,1)} %copy-done.17) | copy-start | bytes 1572868
  64.2 1.3 %collective-permute-start.2 = (bf16[9,16,128]{2,1,0:T(8,128)(2,1)S(1)}, bf16[9,16,128]{2,1,0:T(8,128)(2,1)S(1)}, u32[]{:S(2)}, u32[]{:S(2)}) collective-permute-start(bf16[9,16,128]{2,1,0:T(8,128)(2,1)S(1)} %sums.1), channel_id=1, source_target_pairs={{0,1},{1,0},{2,3},{3,2},{4,5},{5,4},{6,7},{7,6},{8,9},{9,8},{10,11... | collective-permute-start | bytes 110600 | tf_op jit(solution)/shard_map/ppermute | solution.py:375
  65.6 4.9 %copy-start.1 = (bf16[1,2048,128]{2,1,0:T(8,128)(2,1)S(1)}, bf16[1,2048,128]{2,1,0:T(8,128)(2,1)}, u32[]{:S(2)}) copy-start(bf16[1,2048,128]{2,1,0:T(8,128)(2,1)} %param.9) | copy-start | bytes 1572868
  65.6 4.9 %copy-start.2 = (bf16[1,2048,128]{2,1,0:T(8,128)(2,1)S(1)}, bf16[1,2048,128]{2,1,0:T(8,128)(2,1)}, u32[]{:S(2)}) copy-start(bf16[1,2048,128]{2,1,0:T(8,128)(2,1)} %param.10) | copy-start | bytes 1572868
  65.6 4.9 %copy-start.22 = (bf16[128,128]{1,0:T(8,128)(2,1)S(1)}, bf16[128,128]{1,0:T(8,128)(2,1)}, u32[]{:S(2)}) copy-start(bf16[128,128]{1,0:T(8,128)(2,1)} %filters.5) | copy-start | bytes 98308
  67.8 5.2 %collective-permute-start.3 = (bf16[9,16,128]{2,1,0:T(8,128)(2,1)S(1)}, bf16[9,16,128]{2,1,0:T(8,128)(2,1)S(1)}, u32[]{:S(2)}, u32[]{:S(2)}) collective-permute-start(bf16[9,16,128]{2,1,0:T(8,128)(2,1)S(1)} %add_convert_fusion.1), channel_id=1, source_target_pairs={{0,8},{8,0},{16,24},{24,16},{1,9},{9,1},{17,25},{25,17},{2,10},{10... | collective-permute-start | bytes 110600 | tf_op jit(solution)/shard_map/ppermute | solution.py:375
  73.0 4.9 %collective-permute-start.4 = (bf16[9,16,128]{2,1,0:T(8,128)(2,1)S(1)}, bf16[9,16,128]{2,1,0:T(8,128)(2,1)S(1)}, u32[]{:S(2)}, u32[]{:S(2)}) collective-permute-start(bf16[9,16,128]{2,1,0:T(8,128)(2,1)S(1)} %add_convert_fusion.half), channel_id=1, source_target_pairs={{0,16},{8,24},{16,0},{24,8},{1,17},{9,25},{17,1},{25,9},{2,18},{10... | collective-permute-start | bytes 110600 | tf_op jit(solution)/shard_map/ppermute | solution.py:375

commit v2 on v0

v2 whole, which is shorter than its diff:
```python
import functools

import jax
import jax.numpy as jnp
from jax import lax
from jax.experimental import pallas as pl
from jax.experimental.pallas import tpu as pltpu
from jax.sharding import PartitionSpec as P

F32 = jnp.float32
BF16 = jnp.bfloat16
TILE = 128
LANES = 16
PACK = TILE // LANES
CHUNK = 32
STEPS = 4
VMEM_LIMIT = 24 * 1024 * 1024


def nn(lhs, rhs):
    return lax.dot_general(lhs, rhs, (((1,), (0,)), ((), ())), preferred_element_type=F32)


def nt(lhs, rhs):
    return lax.dot_general(lhs, rhs, (((1,), (1,)), ((), ())), preferred_element_type=F32)


def iotas():
    rows = lax.broadcasted_iota(jnp.int32, (TILE, TILE), 0)
    cols = lax.broadcasted_iota(jnp.int32, (TILE, TILE), 1)
    return rows, cols


def ones_where(mask):
    return jnp.where(mask, 1.0, 0.0).astype(BF16)


def column(turned, mask):
    wide = jnp.concatenate([turned] * PACK, axis=0)
    return jnp.sum(jnp.where(mask, wide, 0.0), axis=1, keepdims=True)


def squeeze_groups(wide, mask):
    kept = jnp.where(mask, wide, 0.0)
    total = kept[:LANES]
    for g in range(1, PACK):
        total = total + kept[g * LANES : (g + 1) * LANES]
    return total


def spread_groups(narrow, mask):
    return jnp.where(mask, jnp.concatenate([narrow] * PACK, axis=0), 0.0)


def circulant(row):
    base = jnp.broadcast_to(row, (LANES, TILE))
    base = pltpu.roll(base, 0, 1, stride=1, stride_axis=0).astype(BF16)
    return jnp.concatenate(
        [base] + [pltpu.roll(base, LANES * j, 1) for j in range(1, PACK)], axis=0
    )


def reversal():
    rows, cols = iotas()
    return ones_where((rows + cols) % TILE == 0)


def one_minus_exp(value):
    series = jnp.full_like(value, 1.0)
    for order in (7, 6, 5, 4, 3, 2):
        series = 1.0 - value * series / order
    return jnp.where(value < 0.125, value * series, 1.0 - jnp.exp(-value))


def chunk_mask(shape, bit):
    return (lax.broadcasted_iota(jnp.int32, shape, 1) // CHUNK) & bit == 0


def pair_chunks(turned):
    parts = [turned[CHUNK * j : CHUNK * (j + 1), :] for j in range(TILE // CHUNK)]
    for bit in (1, 2):
        keep = chunk_mask((CHUNK, TILE), bit)
        for j in range(len(parts)):
            if j & bit == 0:
                low, high = parts[j], parts[j + bit]
                parts[j] = jnp.where(keep, low, pltpu.roll(high, CHUNK * bit, 1))
                parts[j + bit] = jnp.where(keep, pltpu.roll(low, TILE - CHUNK * bit, 1), high)
    return parts


def windows(before, now):
    lanes = lax.broadcasted_iota(jnp.int32, now.shape, 1)
    none = jnp.zeros_like(now)
    first, second = [none if before is None else before], [now]
    for j in range(1, TILE // CHUNK):
        left = TILE - CHUNK * j
        moved = pltpu.roll(now, left, 1)
        older = none if before is None else pltpu.roll(before, left, 1)
        first.append(jnp.where(lanes < left, older, moved))
        second.append(moved)
    return jnp.concatenate(
        [jnp.concatenate(first, axis=0), jnp.concatenate(second, axis=0)], axis=1
    )


def beside(first, second):
    return jnp.concatenate([first, second], axis=1)


def above(first, second):
    return jnp.concatenate([first, second], axis=0)


def apart(first, second):
    none = jnp.zeros_like(first)
    return above(beside(first, none), beside(none, second))


def lag_rows(chunks, others, shifted_rows, other_rows, own_rows):
    left = [jnp.concatenate([part * own for own in own_rows], axis=0) for part in (chunks, others)]
    wide = nn(apart(*left), above(shifted_rows, other_rows))
    rows = lax.broadcasted_iota(jnp.int32, wide[:, :TILE].shape, 0) % CHUNK
    lanes = lax.broadcasted_iota(jnp.int32, wide[:, :TILE].shape, 1)
    sums = jnp.where(lanes + rows < CHUNK, wide[:, TILE:], wide[:, :TILE])
    sums = [
        jnp.sum(
            pltpu.roll(sums[CHUNK * i : CHUNK * (i + 1)], 0, 1, stride=1, stride_axis=0),
            axis=0, keepdims=True,
        )
        for i in range(4)
    ]
    return above(*sums[:2]), above(*sums[2:])


def now_and_before(now, before, rows, half):
    both = beside(now, before)
    pieces = []
    for g in range(0, PACK, 2):
        circs = beside(*[circulant(rows[h : h + 1, :]) for h in (g, g + 1)])
        w_now = circs * half
        wide = nn(both[g * LANES : (g + 2) * LANES, :], above(w_now, circs - w_now))
        pieces += [wide[:LANES, :TILE], wide[LANES:, TILE:]]
    return jnp.concatenate(pieces, axis=0)


def within_shard(array, rows, half):
    pieces = []
    for g in range(0, PACK, 4):
        weights = [
            beside(*[circulant(rows[h : h + 1, :]) for h in (k, k + 1)]) * half
            for k in (g, g + 2)
        ]
        parts = [array[k * LANES : (k + 2) * LANES, :] for k in (g, g + 2)]
        wide = nn(apart(*parts), above(*weights))
        for k in range(4):
            column_at = (k % 2) * TILE
            pieces.append(wide[k * LANES : (k + 1) * LANES, column_at : column_at + TILE])
    return jnp.concatenate(pieces, axis=0)


def block_groups(at, blocks, block):
    rows, cols = iotas()
    return cols == rows // LANES + (at * blocks + block) * PACK


def gate_kernel(query, key, product, held, made, arrived, left):
    size = held.shape[1] // STEPS

    def fetch(array, step):
        span = pl.ds(step * size, size)
        return pltpu.make_async_copy(
            (query, key)[array].at[span, :], held.at[array, span, :], arrived.at[array, step]
        )

    def store(step):
        span = pl.ds(step * size, size)
        return pltpu.make_async_copy(made.at[span, :], product.at[span, :], left.at[step])

    for step in range(STEPS):
        for array in range(2):
            fetch(array, step).start()
    for step in range(STEPS):
        for array in range(2):
            fetch(array, step).wait()
        span = pl.ds(step * size, size)
        made[span, :] = held[0, span, :] * held[1, span, :]
        store(step).start()
    for step in range(STEPS):
        store(step).wait()


def state_kernel(grad, value, rate, state, wide_rate):
    rows, cols = iotas()
    offsets = cols.astype(F32)
    mask = rows // LANES == cols // LANES
    at = pl.program_id(0)
    blocks = state.shape[0]
    for block in range(blocks):
        span = pl.ds(block * TILE, TILE)
        rates = column(rate[...], block_groups(at, blocks, block))
        powers = jnp.exp(-rates * offsets).astype(BF16)
        wide_rate[block] = squeeze_groups(jnp.broadcast_to(rates, (TILE, TILE)), mask)
        dz2 = grad[span, :] * value[span, :]
        state[block] = squeeze_groups(nt(powers, dz2), mask).astype(BF16)


def table_kernel(rate, residue, to_next, after, to_end, power, taps, turned):
    rows, cols = iotas()
    offsets = cols.astype(F32)
    lags = ((CHUNK - 1 - cols) % TILE).astype(F32)
    at = pl.program_id(0)
    blocks = power.shape[0] // TILE
    coeffs = residue[...] * jnp.sqrt(one_minus_exp(2.0 * rate[...]))
    filters = []
    for block in range(blocks):
        span = pl.ds(block * TILE, TILE)
        own = block_groups(at, blocks, block)
        rates = column(rate[...], own)
        scale = column(coeffs, own)
        powers = jnp.exp(-rates * offsets)
        scaled = powers * scale
        ends = jnp.exp(-rates * (TILE - 1 - offsets))
        power[span, :] = jnp.exp(-rates * lags).astype(BF16)
        to_end[span, :] = ends.astype(BF16)
        after[span, :] = scaled.astype(BF16)
        to_next[span, :] = (ends * scale).astype(BF16)
        filters.append(jnp.sum(scaled.reshape(PACK, LANES, TILE), axis=1))
    filters = jnp.concatenate(filters, axis=0)
    taps[...] = filters
    turned[...] = nn(filters.astype(BF16), reversal())


def local_kernel(grad, value, turned, du2):
    rows, cols = iotas()
    lower = ones_where(rows >= cols)
    lower_half = beside(lower, lower)
    for block in range(grad.shape[0] // TILE):
        span = pl.ds(block * TILE, TILE)
        dz2 = grad[span, :] * value[span, :]
        du2[span, :] = within_shard(dz2, turned[pl.ds(block * PACK, PACK), :], lower_half)


def middle_kernel(states, local, to_next, li_key, value, dz1, du2):
    rows, cols = iotas()
    mask = rows // LANES == cols // LANES
    for block in range(local.shape[0] // TILE):
        span = pl.ds(block * TILE, TILE)
        wide = spread_groups(states[block], mask).T.astype(BF16)
        total = local[span, :] + nn(wide, to_next[span, :])
        du2[span, :] = total
        dy1 = total * li_key[span, :].astype(F32)
        dz1[span, :] = (dy1 * value[span, :].astype(F32)).astype(BF16)


def forward_kernel(
    before, now, filters, value, li_key, to_end, du2, grad_value, grad_key, u2, state
):
    rows, cols = iotas()
    mask = rows // LANES == cols // LANES
    upper = ones_where(cols >= rows)
    upper_half = beside(upper, upper)
    for block in range(now.shape[0] // TILE):
        span = pl.ds(block * TILE, TILE)
        filt = filters[pl.ds(block * PACK, PACK), :].astype(F32)
        z1 = now_and_before(now[span, :], before[span, :], filt, upper_half)
        y1 = (value[span, :].astype(F32) * z1).astype(BF16).astype(F32)
        key_two = li_key[span, :].astype(F32)
        u2_half = (y1 * key_two).astype(BF16)
        u2[span, :] = u2_half
        state[block] = squeeze_groups(nt(to_end[span, :], u2_half), mask).astype(BF16)
        du2_here = du2[span, :]
        grad_key[span, :] = (du2_here * y1).astype(BF16)
        grad_value[span, :] = (du2_here * key_two * z1).astype(BF16)


def sums_kernel(
    before, now, u2, dz1, grad, li_value, power, state, after_shard, rate,
    packed, filter_sums, within_sums, across_sums,
):
    rows, cols = iotas()
    turn = ones_where(cols == rows - rows % CHUNK + (CHUNK - 1 - rows % CHUNK))
    lanes = lax.broadcasted_iota(jnp.int32, (CHUNK, TILE), 1)
    own_rows = [ones_where((lanes // LANES) % 2 == i) for i in range(2)]
    at = pl.program_id(0)
    blocks = now.shape[0] // TILE

    @pl.when(at == 0)
    def _():
        within_sums[...] = jnp.zeros_like(within_sums)
        across_sums[...] = jnp.zeros_like(across_sums)

    for block in range(blocks):
        span = pl.ds(block * TILE, TILE)
        dz2 = grad[span, :] * li_value[span, :]
        turned = nt(turn, jnp.concatenate([dz1[span, :], dz2], axis=0)).astype(BF16)
        lag_chunks = pair_chunks(turned[:, :TILE])
        energy_chunks = pair_chunks(turned[:, TILE:])
        lags, energies = [], []
        for p in range(TILE // CHUNK):
            pair = pl.ds(block * TILE + p * CHUNK, CHUNK)
            lag, energy = lag_rows(
                lag_chunks[p], energy_chunks[p],
                windows(before[pair, :], now[pair, :]), windows(None, u2[pair, :]), own_rows,
            )
            lags.append(lag)
            energies.append(energy)
        few = pl.ds(pl.multiple_of((at * blocks + block) * PACK, PACK), PACK)
        filter_sums[few, :] = jnp.concatenate(lags, axis=0)
        energies = jnp.concatenate(energies, axis=0).astype(BF16)
        energies = jnp.concatenate([energies] * LANES, axis=0)
        own = block_groups(at, blocks, block)
        within_sums[...] += squeeze_groups(nt(power[span, :], energies), own)
        packed[at * blocks + block] = state[block]
        across = state[block].astype(F32) * after_shard[block]
        across_sums[...] += nn(across.astype(BF16), ones_where(own))

    @pl.when(at == STEPS - 1)
    def _():
        place = ones_where((rows + cols) % TILE == CHUNK - 1)
        sums = nn(filter_sums[...].astype(BF16), place).astype(BF16)
        for chunk in range(filter_sums.shape[0] // LANES):
            packed[STEPS * blocks + chunk] = sums[chunk * LANES : (chunk + 1) * LANES]
        gains = jnp.sqrt(one_minus_exp(2.0 * rate[...]))
        total = gains * (within_sums[...] + across_sums[...])
        packed[STEPS * blocks + filter_sums.shape[0] // LANES] = total.astype(BF16)


def within_kernel(u2, taps, z2):
    rows, cols = iotas()
    upper = ones_where(cols >= rows)
    upper_half = beside(upper, upper)
    for block in range(u2.shape[0] // TILE):
        span = pl.ds(block * TILE, TILE)
        z2[span, :] = within_shard(u2[span, :], taps[pl.ds(block * PACK, PACK), :], upper_half)


def last_kernel(half, other, grad_filter, grad_residue):
    chunks = half.shape[0] - 1
    for chunk in range(chunks):
        grad_filter[pl.ds(chunk * LANES, LANES), :] = half[chunk].astype(F32) + other[chunk].astype(F32)
    grad_residue[...] = half[chunks].astype(F32) + other[chunks].astype(F32)


def product_kernel(dz1, later, filters, query, key, grad_query, grad_key):
    rows, cols = iotas()
    lower = ones_where(rows >= cols)
    lower_half = beside(lower, lower)
    turned = nn(filters[...], reversal())
    for block in range(dz1.shape[0] // TILE):
        span = pl.ds(block * TILE, TILE)
        filt = turned[block * PACK : (block + 1) * PACK]
        du1 = now_and_before(dz1[span, :], later[span, :], filt, lower_half)
        grad_query[span, :] = (du1 * key[span, :].astype(F32)).astype(BF16)
        grad_key[span, :] = (du1 * query[span, :].astype(F32)).astype(BF16)


def value_kernel(states, after, z2, grad, grad_value):
    rows, cols = iotas()
    mask = rows // LANES == cols // LANES
    for block in range(z2.shape[0] // TILE):
        span = pl.ds(block * TILE, TILE)
        wide = spread_groups(states[block], mask).T.astype(BF16)
        total = z2[span, :] + nn(wide, after[span, :])
        grad_value[span, :] = (grad[span, :].astype(F32) * total).astype(BF16)


def shifted(value, axis, steps):
    count = lax.axis_size(axis)
    first, last = max(0, -steps), min(count, count - steps)
    return lax.ppermute(value, axis, [(source, source + steps) for source in range(first, last)])


def swapped(value, axis, bit):
    count = lax.axis_size(axis)
    return lax.ppermute(value, axis, [(source, source ^ bit) for source in range(count)])


def scan_rounds():
    count, bit, bits = lax.axis_size("seq"), 1, []
    assert count & (count - 1) == 0
    while bit < count:
        bits.append(bit)
        bit *= 2
    return bits


def merged(outside, total, other, bit, wide_rate, earlier):
    place = lax.axis_index("seq")
    low = (place & bit) == 0
    at = place & (bit - 1)

    def fade(shards):
        return jnp.exp(-wide_rate * (TILE * shards).astype(F32))

    run = fade(jnp.int32(bit))
    if earlier:
        outside = outside + jnp.where(low, 0.0, fade(at) * other)
        total = jnp.where(low, other + run * total, total + run * other)
    else:
        outside = outside + jnp.where(low, fade(bit - 1 - at) * other, 0.0)
        total = jnp.where(low, total + run * other, other + run * total)
    return outside, total


def per_device(
    mr_query, mr_key, mr_value, li_key, li_value, grad_out, mr_filter, li_residue, li_rate
):
    query, key, value, key_two, value_two, grad = (
        array[0] for array in (mr_query, mr_key, mr_value, li_key, li_value, grad_out)
    )
    groups, filt_len = mr_filter.shape
    channels, seq_local = query.shape
    assert filt_len == TILE and seq_local == TILE and groups <= TILE
    assert channels == groups * LANES and li_rate.shape[1] == LANES
    rows = channels // STEPS
    few = groups // STEPS
    spare = ((0, 0), (0, TILE - groups))
    rate = jnp.pad(li_rate.T, spare)
    residue = jnp.pad(li_residue.T, spare)

    blocks = channels // TILE

    wide = pl.BlockSpec((rows, TILE), lambda i: (i, 0))
    table = pl.BlockSpec((few, TILE), lambda i: (i, 0))
    chunk = pl.BlockSpec((blocks // STEPS, LANES, TILE), lambda i: (i, 0, 0))
    modes = pl.BlockSpec((LANES, TILE), lambda i: (0, 0))
    distant = pl.BlockSpec(memory_space=pltpu.HBM)
    wide_half = jax.ShapeDtypeStruct((channels, TILE), BF16)
    wide_full = jax.ShapeDtypeStruct((channels, TILE), F32)
    table_full = jax.ShapeDtypeStruct((groups, TILE), F32)
    chunk_half = jax.ShapeDtypeStruct((blocks, LANES, TILE), BF16)
    chunk_full = jax.ShapeDtypeStruct((blocks, LANES, TILE), F32)

    def call(kernel, name, in_specs, out_specs, out_shape, scratch=(), grid=STEPS, limit=VMEM_LIMIT):
        return pl.pallas_call(
            kernel,
            grid=(grid,),
            in_specs=in_specs,
            out_specs=out_specs,
            out_shape=out_shape,
            scratch_shapes=scratch,
            name=name,
            cost_estimate=pl.CostEstimate(flops=1, bytes_accessed=1, transcendentals=0),
            compiler_params=pltpu.CompilerParams(vmem_limit_bytes=limit),
        )

    def whole(leaf):
        return pl.BlockSpec(leaf.shape, lambda i: (0,) * len(leaf.shape))

    (product,) = call(
        gate_kernel, "gate", [distant] * 2, [distant], [wide_half],
        [
            pltpu.VMEM((2, channels, TILE), BF16), pltpu.VMEM((channels, TILE), BF16),
            pltpu.SemaphoreType.DMA((2, STEPS)), pltpu.SemaphoreType.DMA((STEPS,)),
        ],
        grid=1, limit=60 * 1024 * 1024,
    )(query, key)
    product_before = shifted(product, "seq", 1)

    grad_kept, _ = lax.optimization_barrier((grad, product))
    back, wide_rate = call(
        state_kernel, "state", [wide, wide, modes], [chunk, chunk], [chunk_half, chunk_full]
    )(grad_kept, value_two, rate)

    def make_tables():
        return call(
            table_kernel, "table", [modes, modes], [wide] * 4 + [table] * 2,
            [wide_half] * 4 + [table_full] * 2,
        )(rate, residue)

    def make_local(tables):
        return call(local_kernel, "local", [wide, wide, table], [wide], [wide_full])(
            grad, value_two, tables[-1]
        )

    outside, total = jnp.zeros(back.shape, F32), back.astype(F32)
    tables, local = None, None
    for bit in scan_rounds():
        other = swapped(total.astype(BF16), "seq", bit).astype(F32)
        outside, total = merged(outside, total, other, bit, wide_rate, False)
        if tables is None:
            tables = make_tables()
            total, tables = lax.optimization_barrier((total, tables))
        elif local is None:
            local = make_local(tables)
    to_next, after, to_end, power, taps, _ = tables
    (du2_local,) = local
    after_shard = outside * jnp.exp(-wide_rate)
    after_shard, product_before = lax.optimization_barrier((after_shard, product_before))

    dz1, du2 = call(
        middle_kernel, "middle", [chunk, wide, wide, wide, wide], [wide, wide],
        [wide_half, wide_full],
    )(after_shard, du2_local, to_next, key_two, value)
    dz1_later = shifted(dz1, "seq", -1)

    grad_mr_value, grad_li_key, u2, state = call(
        forward_kernel, "forward",
        [wide, wide, table, wide, wide, wide, wide],
        [wide, wide, wide, chunk], [wide_half] * 3 + [chunk_half],
    )(product_before, product, mr_filter, value, key_two, to_end, du2)

    filter_chunks = groups // LANES
    packed_shape = jax.ShapeDtypeStruct((blocks + filter_chunks + 1, LANES, TILE), BF16)
    (packed,) = call(
        sums_kernel, "sums",
        [wide] * 7 + [chunk, chunk, modes],
        [whole(packed_shape)], [packed_shape],
        [pltpu.VMEM((groups, TILE), F32)] + [pltpu.VMEM((LANES, TILE), F32)] * 2,
    )(product_before, product, u2, dz1, grad, value_two, power, state, after_shard, rate)

    packed, dz1_later = lax.optimization_barrier((packed, dz1_later))

    def make_within():
        return call(within_kernel, "within", [wide, table], [wide], [wide_full])(u2, taps)

    def make_products():
        return call(
            product_kernel, "product",
            [wide, wide, table, wide, wide], [wide, wide], [wide_half, wide_half],
        )(dz1, dz1_later, mr_filter, query, key)

    outside, total = jnp.zeros(back.shape, F32), packed[:blocks].astype(F32)
    within, products = None, None
    for bit in scan_rounds():
        other = swapped(packed, "seq", bit)
        sums = (packed[blocks:].astype(F32) + other[blocks:].astype(F32)).astype(BF16)
        outside, total = merged(
            outside, total, other[:blocks].astype(F32), bit, wide_rate, True
        )
        if within is None:
            within = make_within()
            total, within = lax.optimization_barrier((total, within))
        elif products is None:
            products = make_products()
            sums, products = lax.optimization_barrier((sums, products))
        packed = jnp.concatenate([total.astype(BF16), sums], axis=0)
    (z2,), (grad_query, grad_key) = within, products
    before_shard = outside * jnp.exp(-wide_rate)

    assert lax.axis_size("dp") == 2
    partner = swapped(sums, "dp", 1)
    (grad_li_value,) = call(
        value_kernel, "value", [chunk, wide, wide, wide], [wide], [wide_half]
    )(before_shard, after, z2, grad)

    residue_full = jax.ShapeDtypeStruct((LANES, TILE), F32)
    grad_filter, grad_residue = call(
        last_kernel, "last", [whole(sums)] * 2,
        [whole(table_full), whole(residue_full)], [table_full, residue_full], grid=1,
    )(sums, partner)
    return (
        grad_query[None],
        grad_key[None],
        grad_mr_value[None],
        grad_li_key[None],
        grad_li_value[None],
        grad_filter,
        grad_residue[:, :groups].T,
    )


def solution(mesh):
    streams = (P("dp", "chan", "seq"),)
    tables = (P("chan", None),)
    return jax.shard_map(
        per_device,
        mesh=mesh,
        in_specs=streams * 6 + tables * 3,
        out_specs=streams * 5 + tables * 2,
        check_vma=False,
    )
```

time: 62.7 us -> 61.4 us (0.979)
  local copies, waits for them, and re-layouts: 0.05 us -> 5.1 us
  starting transfers between devices: 21.7 us -> 16.7 us
  other arithmetic: 0.04 us -> 2.56 us
  waiting for transfers between devices: 6.02 us -> 3.92 us
  Pallas kernels: 33.6 us -> 31.8 us
    ppermute x8 -> x2, starting transfers between devices: 21.5 us -> 3.25 us  [shifted(): lax.ppermute(value, axis, [(source, source + steps) for source in range(f...]
    ppermute x3 -> x5, starting transfers between devices: 0.21 us -> 13.5 us  [swapped(): lax.ppermute(value, axis, [(source, source ^ bit) for source in range(cou...]
    unnamed x20 -> x40, local copies, waits for them, and re-layouts: 0.05 us -> 5.1 us
    ppermute x8 -> x2, waiting for transfers between devices: 3.35 us -> 1.11 us  [shifted(): lax.ppermute(value, axis, [(source, source + steps) for source in range(f...]
    pallas_call x8 -> x10, Pallas kernels: 28.6 us -> 26.8 us  [the longest x1 9.44 us: per_device(): call(sums_kernel, 'sums', [wide] * 7 + [chunk, chunk, modes], [whole(pack...]
    mul x0 -> x2, other arithmetic: none -> 1.01 us  [the longest x1 0.92 us: per_device(): before_shard = outside * jnp.exp(-wide_rate)]
    convert_element_type x2, other arithmetic: 0.04 us -> 0.8 us  [per_device(): (packed[blocks:].astype(F32) + other[blocks:].astype(F32)).astype(BF16)]
    concatenate x0 -> x1, other arithmetic: none -> 0.65 us  [per_device(): packed = jnp.concatenate([total.astype(BF16), sums], axis=0)]
  transfers between devices with their start and end apart: 11 -> 7, of which waited for: 2 -> 3; matrix products, arithmetic and copies ran while one was open for 0% -> 2% of each run, Pallas kernels for 46% -> 44%
where the time goes in v2:
time: 61.4 us; the launch traced here: 61 us
  Pallas kernels  31.8 us (52%)
  starting transfers between devices  16.7 us (27%)
  local copies, waits for them, and re-layouts  5.1 us (8%)
  waiting for transfers between devices  3.92 us (6%)
  other arithmetic  2.56 us (4%)
  between operations  0.91 us (1%)
    ppermute x5, starting transfers between devices, swapped(): lax.ppermute(value, axis, [(source, source ^ bit) for source in range(cou...  13.5 us
    pallas_call x1, Pallas kernels, per_device(): call(sums_kernel, 'sums', [wide] * 7 + [chunk, chunk, modes], [whole(pack...  9.44 us
    unnamed x40, local copies, waits for them, and re-layouts  5.1 us
    pallas_call x1, Pallas kernels, per_device(): call(forward_kernel, 'forward', [wide, wide, table, wide, wide, wide, wid...  5 us
    pallas_call x1, Pallas kernels, make_products(): call(product_kernel, 'product', [wide, wide, table, wide, wide], [wide, w...  4.18 us
    ppermute x2, starting transfers between devices, shifted(): lax.ppermute(value, axis, [(source, source + steps) for source in range(f...  3.25 us
    ppermute x5, waiting for transfers between devices, swapped(): lax.ppermute(value, axis, [(source, source ^ bit) for source in range(cou...  2.81 us
    pallas_call x1, Pallas kernels, make_within(): call(within_kernel, 'within', [wide, table], [wide], [wide_full])(u2, taps)  2.26 us
  transfers between devices with their start and end apart: 7, of which 3 were waited for; matrix products, arithmetic and copies ran while one was open for 2% of the time, Pallas kernels for 44%

profile of v2, /device:TPU:0, one launch (start us, length us, event | category | flops | bytes accessed | tf_op | source)
XLA Modules:
  0.0 61.0 jit_solution(3533030008313530987)
XLA Ops:
  0.6 0.0 copy-start
  0.6 0.0 copy-start.2
  0.7 0.0 copy-start.18
  0.7 2.1 %gate.1.now = bf16[2048,128]{1,0:T(8,128)(2,1)} custom-call(bf16[2048,128]{1,0:T(8,128)(2,1)} %bitcast.25, bf16[2048,128]{1,0:T(8,128)(2,1)} %bitcast.27), custom_call_target="tpu_custom_call" | custom-call | flops 1 | bytes 1 | tf_op jit(solution)/shard_map/gate/pallas_call | solution.py:450
  2.8 0.0 copy-done
  2.8 0.0 copy-start.1
  2.9 0.0 copy-start.19
  2.9 1.2 %state.1 = (bf16[16,16,128]{2,1,0:T(8,128)(2,1)S(1)}, f32[16,16,128]{2,1,0:T(8,128)S(1)}) custom-call(bf16[2048,128]{1,0:T(8,128)(2,1)S(1)} %bitcast.14, bf16[2048,128]{1,0:T(8,128)(2,1)S(1)} %bitcast.18, f32[16,128]{1,0:T(8,128)S(1)} %bitcast.29), custom_call_target="tpu_custom_call" | custom-call | flops 1 | bytes 1 | tf_op jit(solution)/shard_map/state/pallas_call | solution.py:461
  4.0 3.1 %collective-permute-start = (bf16[16,16,128]{2,1,0:T(8,128)(2,1)S(1)}, bf16[16,16,128]{2,1,0:T(8,128)(2,1)S(1)}, u32[]{:S(2)}, u32[]{:S(2)}) collective-permute-start(bf16[16,16,128]{2,1,0:T(8,128)(2,1)S(1)} %get-tuple-element.44), channel_id=1, source_target_pairs={{0,8},{8,0},{16,24},{24,16},{1,9},{9,1},{17,25},{25,17},{2,10},{10... | collective-permute-start | bytes 196616 | tf_op jit(solution)/shard_map/ppermute | solution.py:375
  7.1 2.0 %collective-permute-start.2 = (bf16[2048,128]{1,0:T(8,128)(2,1)S(1)}, bf16[2048,128]{1,0:T(8,128)(2,1)S(1)}, u32[]{:S(2)}, u32[]{:S(2)}) collective-permute-start(bf16[2048,128]{1,0:T(8,128)(2,1)S(1)} %copy-done.1), channel_id=1, source_target_pairs={{0,8},{8,16},{16,24},{1,9},{9,17},{17,25},{2,10},{10,18},{18,26},{... | collective-permute-start | bytes 1572872 | tf_op jit(solution)/shard_map/ppermute | solution.py:370
  9.1 1.5 %table.1 = (bf16[2048,128]{1,0:T(8,128)(2,1)S(1)}, bf16[2048,128]{1,0:T(8,128)(2,1)S(1)}, bf16[2048,128]{1,0:T(8,128)(2,1)S(1)}, bf16[2048,128]{1,0:T(8,128)(2,1...) custom-call(f32[16,128]{1,0:T(8,128)S(1)} %bitcast.30, f32[16,128]{1,0:T(8,128)S(1)} %bitcast.32), custom_call_target="tpu_custom_call" | custom-call | flops 1 | bytes 1 | tf_op jit(solution)/shard_map/table/pallas_call | solution.py:466
  10.6 0.8 %copy-done.7 = bf16[2048,128]{1,0:T(8,128)(2,1)} copy-done((bf16[2048,128]{1,0:T(8,128)(2,1)}, bf16[2048,128]{1,0:T(8,128)(2,1)S(1)}, u32[]{:S(2)}) %copy-start.7) | copy-done | bytes 524312
  11.4 0.8 %copy-done.9 = bf16[2048,128]{1,0:T(8,128)(2,1)} copy-done((bf16[2048,128]{1,0:T(8,128)(2,1)}, bf16[2048,128]{1,0:T(8,128)(2,1)S(1)}, u32[]{:S(2)}) %copy-start.9) | copy-done | bytes 524312
  12.2 0.8 %copy-done.11 = bf16[2048,128]{1,0:T(8,128)(2,1)} copy-done((bf16[2048,128]{1,0:T(8,128)(2,1)}, bf16[2048,128]{1,0:T(8,128)(2,1)S(1)}, u32[]{:S(2)}) %copy-start.11) | copy-done | bytes 524312
  13.0 0.8 %copy-done.13 = bf16[2048,128]{1,0:T(8,128)(2,1)} copy-done((bf16[2048,128]{1,0:T(8,128)(2,1)}, bf16[2048,128]{1,0:T(8,128)(2,1)S(1)}, u32[]{:S(2)}) %copy-start.13) | copy-done | bytes 524312
  13.8 0.0 collective-permute-done
  13.8 0.1 fusion
  13.9 3.0 %collective-permute-start.1 = (bf16[16,16,128]{2,1,0:T(8,128)(2,1)S(1)}, bf16[16,16,128]{2,1,0:T(8,128)(2,1)S(1)}, u32[]{:S(2)}, u32[]{:S(2)}) collective-permute-start(bf16[16,16,128]{2,1,0:T(8,128)(2,1)S(1)} %fusion), channel_id=1, source_target_pairs={{0,16},{8,24},{16,0},{24,8},{1,17},{9,25},{17,1},{25,9},{2,18},{10... | collective-permute-start | bytes 196616 | tf_op jit(solution)/shard_map/ppermute | solution.py:375
  16.9 2.3 %local.1 = f32[2048,128]{1,0:T(8,128)S(1)} custom-call(bf16[2048,128]{1,0:T(8,128)(2,1)S(1)} %bitcast.15, bf16[2048,128]{1,0:T(8,128)(2,1)S(1)} %bitcast.19, f32[128,128]{1,0:T(8,128)S(1)} %get-tuple-element.55.turned), custom_call_target="tpu_custom_call" | custom-call | flops 1 | bytes 1 | tf_op jit(solution)/shard_map/local/pallas_call | solution.py:472
  19.2 2.5 %collective-permute-done.1 = bf16[16,16,128]{2,1,0:T(8,128)(2,1)S(1)} collective-permute-done((bf16[16,16,128]{2,1,0:T(8,128)(2,1)S(1)}, bf16[16,16,128]{2,1,0:T(8,128)(2,1)S(1)}, u32[]{:S(2)}, u32[]{:S(2)}) %collective-permute-start.1) | collective-permute-done | bytes 65568 | tf_op jit(solution)/shard_map/ppermute | solution.py:375
  21.6 0.1 fusion.4.states.after_shard
  21.7 0.0 collective-permute-done.2.before
  21.8 0.0 copy-start.10
  21.8 0.0 copy-start.17
  21.8 1.1 %middle.1 = (bf16[2048,128]{1,0:T(8,128)(2,1)S(1)}, f32[2048,128]{1,0:T(8,128)S(1)}) custom-call(f32[16,16,128]{2,1,0:T(8,128)S(1)} %fusion.4.states.after_shard, f32[2048,128]{1,0:T(8,128)S(1)} %local.1, bf16[2048,128]{1,0:T(8,128)(2,1)S(1)} %copy-done.14, bf16[2048,128]{1,0:T(8,128)(2,1)S(1)} %bitcast.21, bf16[2048,128]{1,0:T(8,128)(2,1)S(1)} %bitcast.23), custom_call_target="tpu_custom_call" | custom-call | flops 1 | bytes 1 | tf_op jit(solution)/shard_map/middle/pallas_call | solution.py:491
  22.9 1.3 %collective-permute-start.3 = (bf16[2048,128]{1,0:T(8,128)(2,1)S(1)}, bf16[2048,128]{1,0:T(8,128)(2,1)S(1)}, u32[]{:S(2)}, u32[]{:S(2)}) collective-permute-start(bf16[2048,128]{1,0:T(8,128)(2,1)S(1)} %get-tuple-element.59.dz1), channel_id=1, source_target_pairs={{8,0},{16,8},{24,16},{9,1},{17,9},{25,17},{10,2},{18,10},{26,18},{... | collective-permute-start | bytes 1572872 | tf_op jit(solution)/shard_map/ppermute | solution.py:370
  24.2 0.0 copy-start.8
  24.2 5.0 %forward.1 = (bf16[2048,128]{1,0:T(8,128)(2,1)}, bf16[2048,128]{1,0:T(8,128)(2,1)}, bf16[2048,128]{1,0:T(8,128)(2,1)S(1)}, bf16[16,16,128]{2,1,0:T(8,128)(2,1)S(1)}) custom-call(bf16[2048,128]{1,0:T(8,128)(2,1)S(1)} %collective-permute-done.2.before, bf16[2048,128]{1,0:T(8,128)(2,1)S(1)} %copy-done.1, bf16[128,128]{1,0:T(8,128)(2,1)S(1)} %copy-done.17, ...), custom_call_target="tpu_custom_call" | custom-call | flops 1 | bytes 1 | tf_op jit(solution)/shard_map/forward/pallas_call | solution.py:497
  29.2 9.4 %sums.1 = bf16[25,16,128]{2,1,0:T(8,128)(2,1)S(1)} custom-call(bf16[2048,128]{1,0:T(8,128)(2,1)S(1)} %collective-permute-done.2.before, bf16[2048,128]{1,0:T(8,128)(2,1)S(1)} %copy-done.1, bf16[2048,128]{1,0:T(8,128)(2,1)S(1)} %get-tuple-element.58.u2, bf16[2048,128]{1,0:T(8,128)(2,1)S(1)} %get-tuple-element.59.dz1, bf16[2048,128]{1,0:T(8,128)(2,1)S(1)} %bitcast.16, ...), custom_call_target="tpu_custom_call" | custom-call | flops 1 | bytes 1 | tf_op jit(solution)/shard_map/sums/pallas_call | solution.py:505
  38.7 1.1 %collective-permute-done.3.later = bf16[2048,128]{1,0:T(8,128)(2,1)S(1)} collective-permute-done((bf16[2048,128]{1,0:T(8,128)(2,1)S(1)}, bf16[2048,128]{1,0:T(8,128)(2,1)S(1)}, u32[]{:S(2)}, u32[]{:S(2)}) %collective-permute-start.3) | collective-permute-done | bytes 524320 | tf_op jit(solution)/shard_map/ppermute | solution.py:370
  39.8 0.8 %copy-done.15 = bf16[2048,128]{1,0:T(8,128)(2,1)} copy-done((bf16[2048,128]{1,0:T(8,128)(2,1)}, bf16[2048,128]{1,0:T(8,128)(2,1)S(1)}, u32[]{:S(2)}) %copy-start.15) | copy-done | bytes 524312
  40.6 3.8 %collective-permute-start.4 = (bf16[25,16,128]{2,1,0:T(8,128)(2,1)S(1)}, bf16[25,16,128]{2,1,0:T(8,128)(2,1)S(1)}, u32[]{:S(2)}, u32[]{:S(2)}) collective-permute-start(bf16[25,16,128]{2,1,0:T(8,128)(2,1)S(1)} %sums.1), channel_id=1, source_target_pairs={{0,8},{8,0},{16,24},{24,16},{1,9},{9,1},{17,25},{25,17},{2,10},{10... | collective-permute-start | bytes 307208 | tf_op jit(solution)/shard_map/ppermute | solution.py:375
  44.4 2.3 %within.1.z2 = f32[2048,128]{1,0:T(8,128)S(1)} custom-call(bf16[2048,128]{1,0:T(8,128)(2,1)S(1)} %get-tuple-element.58.u2, f32[128,128]{1,0:T(8,128)S(1)} %get-tuple-element.63.taps), custom_call_target="tpu_custom_call" | custom-call | flops 1 | bytes 1 | tf_op jit(solution)/shard_map/within/pallas_call | solution.py:515
  46.6 0.0 copy-start.5
  46.6 0.4 collective-permute-done.4
  47.0 0.1 fusion.1
  47.1 0.6 %pad_maximum_fusion = bf16[25,16,128]{2,1,0:T(8,128)(2,1)} fusion(bf16[9,16,128]{2,1,0:T(8,128)(2,1)S(1)} %add_convert_fusion.1, bf16[16,16,128]{2,1,0:T(8,128)(2,1)S(1)} %fusion.1), kind=kLoop, calls=%fused_computation.20 | loop fusion | flops 51200 | bytes 204800 | tf_op jit(solution)/shard_map/concatenate | solution.py:537
  47.7 3.5 %collective-permute-start.5 = (bf16[25,16,128]{2,1,0:T(8,128)(2,1)}, bf16[25,16,128]{2,1,0:T(8,128)(2,1)}, u32[]{:S(2)}, u32[]{:S(2)}) collective-permute-start(bf16[25,16,128]{2,1,0:T(8,128)(2,1)} %pad_maximum_fusion), channel_id=1, source_target_pairs={{0,16},{8,24},{16,0},{24,8},{1,17},{9,25},{17,1},{25,9},{2,18},{10... | collective-permute-start | bytes 307208 | tf_op jit(solution)/shard_map/ppermute | solution.py:375
  51.2 1.0 %copy-done.16 = bf16[2048,128]{1,0:T(8,128)(2,1)S(1)} copy-done((bf16[2048,128]{1,0:T(8,128)(2,1)S(1)}, bf16[2048,128]{1,0:T(8,128)(2,1)}, u32[]{:S(2)}) %copy-start.16) | copy-done | bytes 524312
  52.2 4.2 %product.1 = (bf16[2048,128]{1,0:T(8,128)(2,1)}, bf16[2048,128]{1,0:T(8,128)(2,1)}) custom-call(bf16[2048,128]{1,0:T(8,128)(2,1)S(1)} %get-tuple-element.59.dz1, bf16[2048,128]{1,0:T(8,128)(2,1)S(1)} %copy-done.16, bf16[128,128]{1,0:T(8,128)(2,1)S(1)} %copy-done.17, bf16[2048,128]{1,0:T(8,128)(2,1)S(1)} %bitcast.26, bf16[2048,128]{1,0:T(8,128)(2,1)S(1)} %bitcast.28), custom_call_target="tpu_custom_call" | custom-call | flops 1 | bytes 1 | tf_op jit(solution)/shard_map/product/pallas_call | solution.py:518
  56.4 0.0 collective-permute-done.5
  56.4 0.8 %add_convert_fusion.half = bf16[9,16,128]{2,1,0:T(8,128)(2,1)S(1)} fusion(bf16[9,16,128]{2,1,0:T(8,128)(2,1)S(1)} %add_convert_fusion.1, bf16[25,16,128]{2,1,0:T(8,128)(2,1)} %collective-permute-done.5), kind=kLoop, calls=%fused_computation.21 | loop fusion | flops 73728 | bytes 110592 | tf_op jit(solution)/shard_map/convert_element_type | solution.py:527
  57.2 0.1 collective-permute-start.6
  57.3 0.9 %fusion.7.states = f32[16,16,128]{2,1,0:T(8,128)S(1)} fusion(f32[16,16,128]{2,1,0:T(8,128)S(1)} %get-tuple-element.43, bf16[25,16,128]{2,1,0:T(8,128)(2,1)} %collective-permute-done.5, f32[]{:T(128)S(6)} %convert_element_type.63, pred[]{:T(512)S(6)} %eq.9, pred[]{:T(512)S(6)} %eq.8, bf16[25,16,128]{2,1,0:T(8,128)(2,1)S(1)} %collective-permute-done.4), kind=kLoop, calls=%fused_computation.17 | loop fusion | flops 360448 | bytes 393222 | tf_op jit(solution)/shard_map/mul | solution.py:539
  58.2 0.0 copy-done.12
  58.2 2.1 %value.1 = bf16[2048,128]{1,0:T(8,128)(2,1)} custom-call(f32[16,16,128]{2,1,0:T(8,128)S(1)} %fusion.7.states, bf16[2048,128]{1,0:T(8,128)(2,1)S(1)} %copy-done.12, f32[2048,128]{1,0:T(8,128)S(1)} %within.1.z2, bf16[2048,128]{1,0:T(8,128)(2,1)S(1)} %bitcast.17), custom_call_target="tpu_custom_call" | custom-call | flops 1 | bytes 1 | tf_op jit(solution)/shard_map/value/pallas_call | solution.py:543
  60.3 0.0 collective-permute-done.6.other
  60.3 0.6 %last.1 = (f32[128,128]{1,0:T(8,128)}, f32[16,128]{1,0:T(8,128)}) custom-call(bf16[9,16,128]{2,1,0:T(8,128)(2,1)S(1)} %add_convert_fusion.half, bf16[9,16,128]{2,1,0:T(8,128)(2,1)S(1)} %collective-permute-done.6.other), custom_call_target="tpu_custom_call" | custom-call | flops 1 | bytes 1 | tf_op jit(solution)/shard_map/last/pallas_call | solution.py:548
  (24 shorter events, 0.1 us)
Async XLA Ops:
  0.6 2.2 %copy-start = (bf16[1,2048,128]{2,1,0:T(8,128)(2,1)S(1)}, bf16[1,2048,128]{2,1,0:T(8,128)(2,1)}, u32[]{:S(2)}) copy-start(bf16[1,2048,128]{2,1,0:T(8,128)(2,1)} %param.14) | copy-start | bytes 1572868
  0.6 2.2 %copy-start.2 = (bf16[1,2048,128]{2,1,0:T(8,128)(2,1)S(1)}, bf16[1,2048,128]{2,1,0:T(8,128)(2,1)}, u32[]{:S(2)}) copy-start(bf16[1,2048,128]{2,1,0:T(8,128)(2,1)} %param.13) | copy-start | bytes 1572868
  0.7 2.2 %copy-start.18 = (f32[128,16]{0,1:T(8,128)S(1)}, f32[128,16]{0,1:T(8,128)}, u32[]{:S(2)}) copy-start(f32[128,16]{0,1:T(8,128)} %param.17) | copy-start | bytes 24580
  2.8 4.3 %copy-start.1 = (bf16[2048,128]{1,0:T(8,128)(2,1)S(1)}, bf16[2048,128]{1,0:T(8,128)(2,1)}, u32[]{:S(2)}) copy-start(bf16[2048,128]{1,0:T(8,128)(2,1)} %gate.1.now) | copy-start | bytes 1572868
  2.9 6.2 %copy-start.19 = (f32[128,16]{0,1:T(8,128)S(1)}, f32[128,16]{0,1:T(8,128)}, u32[]{:S(2)}) copy-start(f32[128,16]{0,1:T(8,128)} %param.16) | copy-start | bytes 24580
  4.0 9.8 %collective-permute-start = (bf16[16,16,128]{2,1,0:T(8,128)(2,1)S(1)}, bf16[16,16,128]{2,1,0:T(8,128)(2,1)S(1)}, u32[]{:S(2)}, u32[]{:S(2)}) collective-permute-start(bf16[16,16,128]{2,1,0:T(8,128)(2,1)S(1)} %get-tuple-element.44), channel_id=1, source_target_pairs={{0,8},{8,0},{16,24},{24,16},{1,9},{9,1},{17,25},{25,17},{2,10},{10... | collective-permute-start | bytes 196616 | tf_op jit(solution)/shard_map/ppermute | solution.py:375
  7.1 14.6 %collective-permute-start.2 = (bf16[2048,128]{1,0:T(8,128)(2,1)S(1)}, bf16[2048,128]{1,0:T(8,128)(2,1)S(1)}, u32[]{:S(2)}, u32[]{:S(2)}) collective-permute-start(bf16[2048,128]{1,0:T(8,128)(2,1)S(1)} %copy-done.1), channel_id=1, source_target_pairs={{0,8},{8,16},{16,24},{1,9},{9,17},{17,25},{2,10},{10,18},{18,26},{... | collective-permute-start | bytes 1572872 | tf_op jit(solution)/shard_map/ppermute | solution.py:370
  10.6 0.8 %copy-start.7 = (bf16[2048,128]{1,0:T(8,128)(2,1)}, bf16[2048,128]{1,0:T(8,128)(2,1)S(1)}, u32[]{:S(2)}) copy-start(bf16[2048,128]{1,0:T(8,128)(2,1)S(1)} %get-tuple-element.60.power) | copy-start | bytes 1572868
  11.4 0.8 %copy-start.9 = (bf16[2048,128]{1,0:T(8,128)(2,1)}, bf16[2048,128]{1,0:T(8,128)(2,1)S(1)}, u32[]{:S(2)}) copy-start(bf16[2048,128]{1,0:T(8,128)(2,1)S(1)} %get-tuple-element.53.to_end) | copy-start | bytes 1572868
  12.2 0.8 %copy-start.11 = (bf16[2048,128]{1,0:T(8,128)(2,1)}, bf16[2048,128]{1,0:T(8,128)(2,1)S(1)}, u32[]{:S(2)}) copy-start(bf16[2048,128]{1,0:T(8,128)(2,1)S(1)} %get-tuple-element.72.after) | copy-start | bytes 1572868
  13.0 0.8 %copy-start.13 = (bf16[2048,128]{1,0:T(8,128)(2,1)}, bf16[2048,128]{1,0:T(8,128)(2,1)S(1)}, u32[]{:S(2)}) copy-start(bf16[2048,128]{1,0:T(8,128)(2,1)S(1)} %get-tuple-element.56.to_next) | copy-start | bytes 1572868
  13.9 7.8 %collective-permute-start.1 = (bf16[16,16,128]{2,1,0:T(8,128)(2,1)S(1)}, bf16[16,16,128]{2,1,0:T(8,128)(2,1)S(1)}, u32[]{:S(2)}, u32[]{:S(2)}) collective-permute-start(bf16[16,16,128]{2,1,0:T(8,128)(2,1)S(1)} %fusion), channel_id=1, source_target_pairs={{0,16},{8,24},{16,0},{24,8},{1,17},{9,25},{17,1},{25,9},{2,18},{10... | collective-permute-start | bytes 196616 | tf_op jit(solution)/shard_map/ppermute | solution.py:375
  16.9 4.8 %copy-start.3 = (bf16[1,2048,128]{2,1,0:T(8,128)(2,1)S(1)}, bf16[1,2048,128]{2,1,0:T(8,128)(2,1)}, u32[]{:S(2)}) copy-start(bf16[1,2048,128]{2,1,0:T(8,128)(2,1)} %param.12) | copy-start | bytes 1572868
  16.9 4.8 %copy-start.4 = (bf16[1,2048,128]{2,1,0:T(8,128)(2,1)S(1)}, bf16[1,2048,128]{2,1,0:T(8,128)(2,1)}, u32[]{:S(2)}) copy-start(bf16[1,2048,128]{2,1,0:T(8,128)(2,1)} %param.11) | copy-start | bytes 1572868
  16.9 4.8 %copy-start.14 = (bf16[2048,128]{1,0:T(8,128)(2,1)S(1)}, bf16[2048,128]{1,0:T(8,128)(2,1)}, u32[]{:S(2)}) copy-start(bf16[2048,128]{1,0:T(8,128)(2,1)} %copy-done.13) | copy-start | bytes 1572868
  21.8 2.4 %copy-start.10 = (bf16[2048,128]{1,0:T(8,128)(2,1)S(1)}, bf16[2048,128]{1,0:T(8,128)(2,1)}, u32[]{:S(2)}) copy-start(bf16[2048,128]{1,0:T(8,128)(2,1)} %copy-done.9) | copy-start | bytes 1572868
  21.8 2.4 %copy-start.17 = (bf16[128,128]{1,0:T(8,128)(2,1)S(1)}, bf16[128,128]{1,0:T(8,128)(2,1)}, u32[]{:S(2)}) copy-start(bf16[128,128]{1,0:T(8,128)(2,1)} %filters.3) | copy-start | bytes 98308
  22.9 16.9 %collective-permute-start.3 = (bf16[2048,128]{1,0:T(8,128)(2,1)S(1)}, bf16[2048,128]{1,0:T(8,128)(2,1)S(1)}, u32[]{:S(2)}, u32[]{:S(2)}) collective-permute-start(bf16[2048,128]{1,0:T(8,128)(2,1)S(1)} %get-tuple-element.59.dz1), channel_id=1, source_target_pairs={{8,0},{16,8},{24,16},{9,1},{17,9},{25,17},{10,2},{18,10},{26,18},{... | collective-permute-start | bytes 1572872 | tf_op jit(solution)/shard_map/ppermute | solution.py:370
  24.2 5.0 %copy-start.8 = (bf16[2048,128]{1,0:T(8,128)(2,1)S(1)}, bf16[2048,128]{1,0:T(8,128)(2,1)}, u32[]{:S(2)}) copy-start(bf16[2048,128]{1,0:T(8,128)(2,1)} %copy-done.7) | copy-start | bytes 1572868
  39.8 0.8 %copy-start.15 = (bf16[2048,128]{1,0:T(8,128)(2,1)}, bf16[2048,128]{1,0:T(8,128)(2,1)S(1)}, u32[]{:S(2)}) copy-start(bf16[2048,128]{1,0:T(8,128)(2,1)S(1)} %collective-permute-done.3.later) | copy-start | bytes 1572868
  40.6 6.4 %collective-permute-start.4 = (bf16[25,16,128]{2,1,0:T(8,128)(2,1)S(1)}, bf16[25,16,128]{2,1,0:T(8,128)(2,1)S(1)}, u32[]{:S(2)}, u32[]{:S(2)}) collective-permute-start(bf16[25,16,128]{2,1,0:T(8,128)(2,1)S(1)} %sums.1), channel_id=1, source_target_pairs={{0,8},{8,0},{16,24},{24,16},{1,9},{9,1},{17,25},{25,17},{2,10},{10... | collective-permute-start | bytes 307208 | tf_op jit(solution)/shard_map/ppermute | solution.py:375
  44.4 6.8 %copy-start.6 = (bf16[1,2048,128]{2,1,0:T(8,128)(2,1)S(1)}, bf16[1,2048,128]{2,1,0:T(8,128)(2,1)}, u32[]{:S(2)}) copy-start(bf16[1,2048,128]{2,1,0:T(8,128)(2,1)} %param.10) | copy-start | bytes 1572868
  46.6 4.6 %copy-start.5 = (bf16[1,2048,128]{2,1,0:T(8,128)(2,1)S(1)}, bf16[1,2048,128]{2,1,0:T(8,128)(2,1)}, u32[]{:S(2)}) copy-start(bf16[1,2048,128]{2,1,0:T(8,128)(2,1)} %param.9) | copy-start | bytes 1572868
  47.7 8.7 %collective-permute-start.5 = (bf16[25,16,128]{2,1,0:T(8,128)(2,1)}, bf16[25,16,128]{2,1,0:T(8,128)(2,1)}, u32[]{:S(2)}, u32[]{:S(2)}) collective-permute-start(bf16[25,16,128]{2,1,0:T(8,128)(2,1)} %pad_maximum_fusion), channel_id=1, source_target_pairs={{0,16},{8,24},{16,0},{24,8},{1,17},{9,25},{17,1},{25,9},{2,18},{10... | collective-permute-start | bytes 307208 | tf_op jit(solution)/shard_map/ppermute | solution.py:375
  51.2 1.0 %copy-start.16 = (bf16[2048,128]{1,0:T(8,128)(2,1)S(1)}, bf16[2048,128]{1,0:T(8,128)(2,1)}, u32[]{:S(2)}) copy-start(bf16[2048,128]{1,0:T(8,128)(2,1)} %copy-done.15) | copy-start | bytes 1572868
  52.2 6.0 %copy-start.12 = (bf16[2048,128]{1,0:T(8,128)(2,1)S(1)}, bf16[2048,128]{1,0:T(8,128)(2,1)}, u32[]{:S(2)}) copy-start(bf16[2048,128]{1,0:T(8,128)(2,1)} %copy-done.11) | copy-start | bytes 1572868
  57.2 3.1 %collective-permute-start.6 = (bf16[9,16,128]{2,1,0:T(8,128)(2,1)S(1)}, bf16[9,16,128]{2,1,0:T(8,128)(2,1)S(1)}, u32[]{:S(2)}, u32[]{:S(2)}) collective-permute-start(bf16[9,16,128]{2,1,0:T(8,128)(2,1)S(1)} %add_convert_fusion.half), channel_id=1, source_target_pairs={{0,1},{1,0},{2,3},{3,2},{4,5},{5,4},{6,7},{7,6},{8,9},{9,8},{10,11... | collective-permute-start | bytes 110600 | tf_op jit(solution)/shard_map/ppermute | solution.py:375
